TPU v7x, 512 devices: a whole 4x8x8 slice. The times are simulated.
512 devices in a mesh: seq: 128 (over z, x_lo, y), mp: 4 (over x_hi, core).
Axes of the slice: x: 4 (x_hi: 2, x_lo: 2; x = x_hi * 2 + x_lo), y: 8, z: 8, core: 2. Of those that a mesh axis runs over, the one named last changes fastest.
Arguments:
- hidden_entry_states: bfloat16 [16384, 512], P('seq'), may hold values from -6 to 6
- base_ids: int32 [16384], P('seq'), may hold values from 0 to 4
- mask_index: int32 [2048], P('seq'), may hold values from 0 to 16383, as said below
- first_kernel: bfloat16 [9, 512, 512], P(None, None, 'mp'), may hold values from -0.09375 to 0.09375
- second_kernel: bfloat16 [9, 512, 512], P(None, None, 'mp'), may hold values from -0.09375 to 0.09375
- head_weight: bfloat16 [512, 5], replicated, may hold values from -0.5 to 0.5
Outputs:
- input_grad: bfloat16 [16384, 512], P('seq')
- first_kernel_gradient: float32 [9, 512, 512], P(None, 'seq', 'mp')
- second_kernel_gradient: float32 [9, 512, 512], P(None, 'seq', 'mp')
Inputs may be any that keep to these rules, and one draw needn't show every extreme that they name: `mask_index`: each device's 16 entries are distinct positions within its own block of 128 bases, in no particular order.
All inputs are finite; a program needn't handle non-finite values.
Results may differ from a plain program's by a relative error of at most 0.014.
Values may be sent and summed in bfloat16 or wider, within the bound.
A program may use at most 64 MiB of HBM per device.

v0:
```python
import jax
import jax.numpy as jnp
from jax import lax
from jax.sharding import PartitionSpec as P

DILATION_FIRST1 = 2048
DILATION_SECOND2 = 4096


epsilon = 1e-05
root_half = 0.7071067811865476
inv_root_two_pi = 0.3989422804014327


def shifted(x, axis, by):
    peers = lax.axis_size(axis)
    pairs = [(i, i + by) for i in range(peers) if 0 <= i + by < peers]
    return lax.ppermute(x, axis, pairs)


def gelu_parts(conv_out):
    normal_cdf = 0.5 * (1.0 + lax.erf(conv_out * root_half))
    gelu_slope = normal_cdf + conv_out * inv_root_two_pi * jnp.exp(-0.5 * conv_out * conv_out)
    return (conv_out * normal_cdf, gelu_slope)


def norm_parts(activation):
    values = activation.astype(jnp.float32)
    centre = jnp.mean(values, axis=-1, keepdims=True)
    centred = values - centre
    spread = jnp.mean(centred * centred, axis=-1, keepdims=True)
    inverse = lax.rsqrt(spread + epsilon)
    return (centred * inverse, inverse)


def loss_grad(hidden_top, targets, head_weight):
    logits = lax.dot_general(
        head_weight, hidden_top, (((0,), (1,)), ((), ())), preferred_element_type=jnp.float32
    )
    exponent = jnp.exp(logits)
    probability = exponent / jnp.sum(exponent, axis=0, keepdims=True)
    vocab_rows = lax.broadcasted_iota(jnp.int32, logits.shape, 0)
    onehot = (vocab_rows == targets[None, :]).astype(jnp.float32)
    weight = (targets >= 0).astype(jnp.float32)[None, :]
    dlogits = weight * (probability - onehot)
    return lax.dot_general(
        dlogits,
        head_weight.astype(jnp.float32),
        (((0,), (1,)), ((), ())),
        precision=lax.Precision.HIGHEST,
    )


def local(hidden_entry_states, base_ids, mask_index, first_kernel, second_kernel, head_weight):
    seq_count = lax.axis_size("seq")
    rows_per_block = hidden_entry_states.shape[0]
    channels = hidden_entry_states.shape[1]
    own_width = first_kernel.shape[2]
    tap_count = first_kernel.shape[0]
    centre_tap = tap_count // 2
    mask_count = mask_index.shape[0]
    device_row = lax.axis_index("seq")
    block_start = device_row * rows_per_block
    offsets = mask_index - block_start
    positions = lax.broadcasted_iota(jnp.int32, (rows_per_block, mask_count), 0)
    masked = jnp.any(positions == offsets[None, :], axis=1)
    targets = jnp.where(masked, base_ids, -1)

    def forward_conv(source, kernel, dilation_blocks):
        partial_value = jnp.einsum(
            "rd,kdo->kro", source, kernel, preferred_element_type=jnp.float32
        )
        summed = partial_value[centre_tap]
        for tap_index in range(tap_count):
            device_hop = dilation_blocks * (tap_index - centre_tap)
            if device_hop != 0 and abs(device_hop) < seq_count:
                summed = summed + shifted(partial_value[tap_index], "seq", -device_hop)
        return summed

    def tap_sources(grad_conv, dilation_blocks):
        pieces = []
        for tap_index in range(tap_count):
            device_hop = dilation_blocks * (tap_index - centre_tap)
            if device_hop == 0:
                pieces.append(grad_conv)
            elif abs(device_hop) >= seq_count:
                pieces.append(jnp.zeros_like(grad_conv))
            else:
                pieces.append(shifted(grad_conv, "seq", device_hop))
        return jnp.stack(pieces, axis=0)

    def block_forward_pass(source, kernel, dilation_blocks):
        conv_out = forward_conv(source, kernel, dilation_blocks)
        activation, gelu_slope = gelu_parts(conv_out)
        mixed_all = lax.all_gather(activation.astype(jnp.bfloat16), "mp", axis=1, tiled=True)
        normed, inverse = norm_parts(mixed_all)
        result = (source.astype(jnp.float32) + normed).astype(jnp.bfloat16)
        return (result, (source, normed, inverse, gelu_slope))

    def block_backward_pass(grad_out, saved, kernel, dilation_blocks):
        source, normed, inverse, gelu_slope = saved
        mean_grad = jnp.mean(grad_out, axis=-1, keepdims=True)
        mean_cross = jnp.mean(grad_out * normed, axis=-1, keepdims=True)
        grad_act = inverse * (grad_out - mean_grad - normed * mean_cross)
        own_cols = lax.dynamic_slice_in_dim(
            grad_act, lax.axis_index("mp") * own_width, own_width, 1
        )
        grad_conv = (own_cols * gelu_slope).astype(jnp.bfloat16)
        tap_stack = tap_sources(grad_conv, dilation_blocks)
        input_part = jnp.einsum(
            "kro,kdo->rd", tap_stack, kernel, preferred_element_type=jnp.float32
        )
        grad_in = grad_out + lax.psum(input_part.astype(jnp.bfloat16), "mp").astype(jnp.float32)
        kernel_part = jnp.einsum(
            "rd,kro->kdo", source, tap_stack, preferred_element_type=jnp.float32
        )
        by_owner = kernel_part.reshape(tap_count, seq_count, channels // seq_count, own_width)
        received = lax.all_to_all(
            by_owner.astype(jnp.bfloat16), "seq", split_axis=1, concat_axis=1, tiled=True
        ).astype(by_owner.dtype)
        return (grad_in, jnp.sum(received, axis=1))

    first_receptive_span = DILATION_FIRST1 // rows_per_block
    second_receptive_span = DILATION_SECOND2 // rows_per_block
    hidden_after_first, first_residuals = block_forward_pass(
        hidden_entry_states, first_kernel, first_receptive_span
    )
    hidden_after_second, second_residuals = block_forward_pass(
        hidden_after_first, second_kernel, second_receptive_span
    )
    gradient_after_second = loss_grad(hidden_after_second, targets, head_weight)
    gradient_after_first, second_kernel_gradient = block_backward_pass(
        gradient_after_second, second_residuals, second_kernel, second_receptive_span
    )
    gradient_before_first, first_kernel_gradient = block_backward_pass(
        gradient_after_first, first_residuals, first_kernel, first_receptive_span
    )
    input_grad = gradient_before_first.astype(jnp.bfloat16)
    return (input_grad, first_kernel_gradient, second_kernel_gradient)


def solution(mesh):
    placed = (P("seq", None), P("seq"), P("seq"), P(None, None, "mp"), P(None, None, "mp"), P())
    return jax.shard_map(
        local,
        mesh=mesh,
        in_specs=placed,
        out_specs=(P("seq", None), P(None, "seq", "mp"), P(None, "seq", "mp")),
        check_vma=False,
    )
```

profile of v0, /device:TPU:1, one launch (start us, length us, event | category | flops | bytes accessed | tf_op | source)
XLA Modules:
  0.0 294.8 jit_solution(10878889787662550888)
XLA Ops:
  7.2 1.9 convolution_bitcast_fusion.1
  9.2 11.5 %collective-permute-start = (f32[128,128]{0,1:T(8,128)S(1)}, f32[128,128]{0,1:T(8,128)S(1)}, u32[]{:S(2)}, u32[]{:S(2)}) collective-permute-start(f32[128,128]{0,1:T(8,128)S(1)} %get-tuple-element.30), channel_id=1, source_target_pairs={{0,256},{4,260},{8,264},{12,268},{16,272},{20,276},{24,280},{28,28... | collective-permute-start | bytes 196616 | tf_op jit(solution)/shard_map/ppermute | solution.py:18
  20.6 1.3 collective-permute-start.7
  21.9 1.3 collective-permute-start.6
  23.2 1.3 collective-permute-start.5
  24.5 1.3 collective-permute-start.4
  25.9 4.0 %collective-permute-start.3 = (f32[128,128]{0,1:T(8,128)S(1)}, f32[128,128]{0,1:T(8,128)S(1)}, u32[]{:S(2)}, u32[]{:S(2)}) collective-permute-start(f32[128,128]{0,1:T(8,128)S(1)} %get-tuple-element.35), channel_id=1, source_target_pairs={{0,64},{4,68},{8,72},{12,76},{16,80},{20,84},{24,88},{28,92},{32,9... | collective-permute-start | bytes 196616 | tf_op jit(solution)/shard_map/ppermute | solution.py:18
  30.3 4.8 %collective-permute-start.2 = (f32[128,128]{0,1:T(8,128)S(1)}, f32[128,128]{0,1:T(8,128)S(1)}, u32[]{:S(2)}, u32[]{:S(2)}) collective-permute-start(f32[128,128]{0,1:T(8,128)S(1)} %get-tuple-element.36), channel_id=1, source_target_pairs={{0,128},{4,132},{8,136},{12,140},{16,144},{20,148},{24,152},{28,15... | collective-permute-start | bytes 196616 | tf_op jit(solution)/shard_map/ppermute | solution.py:18
  35.1 7.0 %collective-permute-start.1 = (f32[128,128]{0,1:T(8,128)S(1)}, f32[128,128]{0,1:T(8,128)S(1)}, u32[]{:S(2)}, u32[]{:S(2)}) collective-permute-start(f32[128,128]{0,1:T(8,128)S(1)} %get-tuple-element.37), channel_id=1, source_target_pairs={{0,192},{4,196},{8,200},{12,204},{16,208},{20,212},{24,216},{28,22... | collective-permute-start | bytes 196616 | tf_op jit(solution)/shard_map/ppermute | solution.py:18
  44.1 9.7 %all_gather.6 = bf16[128,512]{0,1:T(8,128)(2,1)S(1)} all-gather(bf16[128,128]{0,1:T(8,128)(2,1)S(1)} %get-tuple-element.22), channel_id=1, replica_groups=mesh['seq'=128,'mp'=4] {'mp'}, dimensions={1}, use_global_device_ids=true | all-gather | bytes 163840 | tf_op jit(solution)/shard_map/all_gather | solution.py:95
  55.8 6.9 %collective-permute-start.8 = (f32[128,128]{0,1:T(8,128)S(1)}, f32[128,128]{0,1:T(8,128)S(1)}, u32[]{:S(2)}, u32[]{:S(2)}) collective-permute-start(f32[128,128]{0,1:T(8,128)S(1)} %get-tuple-element.24), channel_id=1, source_target_pairs={{0,384},{4,388},{8,392},{12,396},{16,400},{20,404},{24,408},{28,41... | collective-permute-start | bytes 196616 | tf_op jit(solution)/shard_map/ppermute | solution.py:18
  62.9 1.3 collective-permute-start.13
  64.2 1.3 collective-permute-start.12
  65.5 1.3 collective-permute-start.11
  66.8 4.9 %collective-permute-start.10 = (f32[128,128]{0,1:T(8,128)S(1)}, f32[128,128]{0,1:T(8,128)S(1)}, u32[]{:S(2)}, u32[]{:S(2)}) collective-permute-start(f32[128,128]{0,1:T(8,128)S(1)} %get-tuple-element.28), channel_id=1, source_target_pairs={{0,128},{4,132},{8,136},{12,140},{16,144},{20,148},{24,152},{28,15... | collective-permute-start | bytes 196616 | tf_op jit(solution)/shard_map/ppermute | solution.py:18
  71.7 7.9 %collective-permute-start.9 = (f32[128,128]{0,1:T(8,128)S(1)}, f32[128,128]{0,1:T(8,128)S(1)}, u32[]{:S(2)}, u32[]{:S(2)}) collective-permute-start(f32[128,128]{0,1:T(8,128)S(1)} %get-tuple-element.29), channel_id=1, source_target_pairs={{0,256},{4,260},{8,264},{12,268},{16,272},{20,276},{24,280},{28,28... | collective-permute-start | bytes 196616 | tf_op jit(solution)/shard_map/ppermute | solution.py:18
  79.6 1.2 collective-permute-done.9
  80.9 8.9 %all_gather.7 = bf16[128,512]{0,1:T(8,128)(2,1)S(1)} all-gather(bf16[128,128]{0,1:T(8,128)(2,1)S(1)} %get-tuple-element.20), channel_id=1, replica_groups=mesh['seq'=128,'mp'=4] {'mp'}, dimensions={1}, use_global_device_ids=true | all-gather | bytes 163840 | tf_op jit(solution)/shard_map/all_gather | solution.py:95
  90.9 1.3 collective-permute-start.14
  92.2 6.1 %collective-permute-start.19 = (bf16[128,128]{0,1:T(8,128)(2,1)S(1)}, bf16[128,128]{0,1:T(8,128)(2,1)S(1)}, u32[]{:S(2)}, u32[]{:S(2)}) collective-permute-start(bf16[128,128]{0,1:T(8,128)(2,1)S(1)} %fusion.19), channel_id=1, source_target_pairs={{0,384},{4,388},{8,392},{12,396},{16,400},{20,404},{24,408},{28,41... | collective-permute-start | bytes 98312 | tf_op jit(solution)/shard_map/ppermute | solution.py:18
  98.3 1.8 collective-permute-start.18
  100.2 3.4 %collective-permute-start.17 = (bf16[128,128]{0,1:T(8,128)(2,1)S(1)}, bf16[128,128]{0,1:T(8,128)(2,1)S(1)}, u32[]{:S(2)}, u32[]{:S(2)}) collective-permute-start(bf16[128,128]{0,1:T(8,128)(2,1)S(1)} %fusion.19), channel_id=1, source_target_pairs={{0,128},{4,132},{8,136},{12,140},{16,144},{20,148},{24,152},{28,15... | collective-permute-start | bytes 98312 | tf_op jit(solution)/shard_map/ppermute | solution.py:18
  103.6 1.3 collective-permute-start.16
  104.9 1.3 collective-permute-start.15
  106.3 7.3 %collective-permute-done.15 = bf16[128,128]{0,1:T(8,128)(2,1)S(1)} collective-permute-done((bf16[128,128]{0,1:T(8,128)(2,1)S(1)}, bf16[128,128]{0,1:T(8,128)(2,1)S(1)}, u32[]{:S(2)}, u32[]{:S(2)}) %collective-permute-start.15) | collective-permute-done | bytes 32800 | tf_op jit(solution)/shard_map/ppermute | solution.py:18
  113.6 1.1 fusion.2
  116.0 1.5 copy.69
  117.5 13.0 %all-to-all-start.1 = ((bf16[9,128,4,128]{3,2,0,1:T(4,128)(2,1)}), bf16[9,128,4,128]{3,2,0,1:T(4,128)(2,1)S(1)}, u32[]{:S(2)}, u32[]{:S(2)}) async-start(bf16[9,128,4,128]{3,2,0,1:T(4,128)(2,1)} %copy.69), calls=%async_computation.1 | async-start | bytes 2359296 | tf_op jit(solution)/shard_map/all_to_all | solution.py:118
  130.5 37.6 %all-reduce.3.cloned.1.call-done = bf16[128,512]{0,1:T(8,128)(2,1)} async-done(((bf16[128,512]{0,1:T(8,128)(2,1)}), bf16[128,512]{0,1:T(8,128)(2,1)}) %all-reduce.3.cloned.1.call-update) | async-done | bytes 131088 | tf_op jit(solution)/shard_map/psum | solution.py:113
  170.7 1.3 collective-permute-start.20
  172.0 7.9 %collective-permute-start.27 = (bf16[128,128]{0,1:T(8,128)(2,1)S(1)}, bf16[128,128]{0,1:T(8,128)(2,1)S(1)}, u32[]{:S(2)}, u32[]{:S(2)}) collective-permute-start(bf16[128,128]{0,1:T(8,128)(2,1)S(1)} %fusion.24), channel_id=1, source_target_pairs={{0,256},{4,260},{8,264},{12,268},{16,272},{20,276},{24,280},{28,28... | collective-permute-start | bytes 98312 | tf_op jit(solution)/shard_map/ppermute | solution.py:18
  179.9 5.4 %collective-permute-start.26 = (bf16[128,128]{0,1:T(8,128)(2,1)S(1)}, bf16[128,128]{0,1:T(8,128)(2,1)S(1)}, u32[]{:S(2)}, u32[]{:S(2)}) collective-permute-start(bf16[128,128]{0,1:T(8,128)(2,1)S(1)} %fusion.24), channel_id=1, source_target_pairs={{0,192},{4,196},{8,200},{12,204},{16,208},{20,212},{24,216},{28,22... | collective-permute-start | bytes 98312 | tf_op jit(solution)/shard_map/ppermute | solution.py:18
  185.2 1.3 collective-permute-start.25
  186.5 2.8 collective-permute-start.24
  189.4 1.3 collective-permute-start.21
  190.7 5.1 %collective-permute-done.21 = bf16[128,128]{0,1:T(8,128)(2,1)S(1)} collective-permute-done((bf16[128,128]{0,1:T(8,128)(2,1)S(1)}, bf16[128,128]{0,1:T(8,128)(2,1)S(1)}, u32[]{:S(2)}, u32[]{:S(2)}) %collective-permute-start.21) | collective-permute-done | bytes 32800 | tf_op jit(solution)/shard_map/ppermute | solution.py:18
  195.8 1.3 collective-permute-start.22
  197.1 4.2 %collective-permute-done.22 = bf16[128,128]{0,1:T(8,128)(2,1)S(1)} collective-permute-done((bf16[128,128]{0,1:T(8,128)(2,1)S(1)}, bf16[128,128]{0,1:T(8,128)(2,1)S(1)}, u32[]{:S(2)}, u32[]{:S(2)}) %collective-permute-start.22) | collective-permute-done | bytes 32800 | tf_op jit(solution)/shard_map/ppermute | solution.py:18
  201.4 1.3 collective-permute-start.23
  202.7 3.5 %collective-permute-done.23 = bf16[128,128]{0,1:T(8,128)(2,1)S(1)} collective-permute-done((bf16[128,128]{0,1:T(8,128)(2,1)S(1)}, bf16[128,128]{0,1:T(8,128)(2,1)S(1)}, u32[]{:S(2)}, u32[]{:S(2)}) %collective-permute-start.23) | collective-permute-done | bytes 32800 | tf_op jit(solution)/shard_map/ppermute | solution.py:18
  207.1 1.4 fusion
  208.5 1.7 copy.65
  210.2 1.4 copy.66
  211.6 11.4 %all-to-all-start = ((bf16[9,128,4,128]{3,2,0,1:T(4,128)(2,1)}), bf16[9,128,4,128]{3,2,0,1:T(4,128)(2,1)S(1)}, u32[]{:S(2)}, u32[]{:S(2)}) async-start(bf16[9,128,4,128]{3,2,0,1:T(4,128)(2,1)} %copy.66), calls=%async_computation | async-start | bytes 2359296 | tf_op jit(solution)/shard_map/all_to_all | solution.py:118
  223.1 2.5 fusion.3
  225.6 56.8 %all-reduce.5.cloned.1.call-done = bf16[128,512]{0,1:T(8,128)(2,1)} async-done(((bf16[128,512]{0,1:T(8,128)(2,1)}), bf16[128,512]{0,1:T(8,128)(2,1)}) %all-reduce.5.cloned.1.call-update) | async-done | bytes 131088 | tf_op jit(solution)/shard_map/psum | solution.py:113
  282.4 1.7 add_convert_fusion
  284.0 1.7 copy.70
  (105 shorter events, 12.7 us)
Async XLA Ops:
  7.2 48.0 %copy-start = (bf16[9,512,128]{2,1,0:T(8,128)(2,1)S(1)}, bf16[9,512,128]{2,1,0:T(8,128)(2,1)}, u32[]{:S(2)}) copy-start(bf16[9,512,128]{2,1,0:T(8,128)(2,1)} %param.10) | copy-start | bytes 3538948
  7.2 35.0 %copy-start.7 = (bf16[128,512]{1,0:T(8,128)(2,1)S(1)}, bf16[128,512]{1,0:T(8,128)(2,1)}, u32[]{:S(2)}) copy-start(bf16[128,512]{1,0:T(8,128)(2,1)} %param.6) | copy-start | bytes 393220
  7.2 34.9 %copy-start.12 = (s32[16]{0:T(128)S(1)}, s32[16]{0:T(128)}, u32[]{:S(2)}) copy-start(s32[16]{0:T(128)} %param.8) | copy-start | bytes 196
  7.2 160.8 %all-reduce.3.cloned.1.call-start = ((), (), s32[]{:S(2)}) async-start(), calls=%async_computation.2 | async-start | bytes 262144 | tf_op jit(solution)/shard_map/psum | solution.py:113
  9.2 16.7 %collective-permute-start = (f32[128,128]{0,1:T(8,128)S(1)}, f32[128,128]{0,1:T(8,128)S(1)}, u32[]{:S(2)}, u32[]{:S(2)}) collective-permute-start(f32[128,128]{0,1:T(8,128)S(1)} %get-tuple-element.30), channel_id=1, source_target_pairs={{0,256},{4,260},{8,264},{12,268},{16,272},{20,276},{24,280},{28,28... | collective-permute-start | bytes 196616 | tf_op jit(solution)/shard_map/ppermute | solution.py:18
  20.6 9.6 %collective-permute-start.7 = (f32[128,128]{0,1:T(8,128)S(1)}, f32[128,128]{0,1:T(8,128)S(1)}, u32[]{:S(2)}, u32[]{:S(2)}) collective-permute-start(f32[128,128]{0,1:T(8,128)S(1)} %get-tuple-element.31), channel_id=1, source_target_pairs={{256,0},{260,4},{264,8},{268,12},{272,16},{276,20},{280,24},{284,2... | collective-permute-start | bytes 196616 | tf_op jit(solution)/shard_map/ppermute | solution.py:18
  21.9 13.2 %collective-permute-start.6 = (f32[128,128]{0,1:T(8,128)S(1)}, f32[128,128]{0,1:T(8,128)S(1)}, u32[]{:S(2)}, u32[]{:S(2)}) collective-permute-start(f32[128,128]{0,1:T(8,128)S(1)} %get-tuple-element.32), channel_id=1, source_target_pairs={{192,0},{196,4},{200,8},{204,12},{208,16},{212,20},{216,24},{220,2... | collective-permute-start | bytes 196616 | tf_op jit(solution)/shard_map/ppermute | solution.py:18
  23.2 19.1 %collective-permute-start.5 = (f32[128,128]{0,1:T(8,128)S(1)}, f32[128,128]{0,1:T(8,128)S(1)}, u32[]{:S(2)}, u32[]{:S(2)}) collective-permute-start(f32[128,128]{0,1:T(8,128)S(1)} %get-tuple-element.33), channel_id=1, source_target_pairs={{128,0},{132,4},{136,8},{140,12},{144,16},{148,20},{152,24},{156,2... | collective-permute-start | bytes 196616 | tf_op jit(solution)/shard_map/ppermute | solution.py:18
  24.5 17.8 %collective-permute-start.4 = (f32[128,128]{0,1:T(8,128)S(1)}, f32[128,128]{0,1:T(8,128)S(1)}, u32[]{:S(2)}, u32[]{:S(2)}) collective-permute-start(f32[128,128]{0,1:T(8,128)S(1)} %get-tuple-element.34), channel_id=1, source_target_pairs={{64,0},{68,4},{72,8},{76,12},{80,16},{84,20},{88,24},{92,28},{96,3... | collective-permute-start | bytes 196616 | tf_op jit(solution)/shard_map/ppermute | solution.py:18
  25.9 16.5 %collective-permute-start.3 = (f32[128,128]{0,1:T(8,128)S(1)}, f32[128,128]{0,1:T(8,128)S(1)}, u32[]{:S(2)}, u32[]{:S(2)}) collective-permute-start(f32[128,128]{0,1:T(8,128)S(1)} %get-tuple-element.35), channel_id=1, source_target_pairs={{0,64},{4,68},{8,72},{12,76},{16,80},{20,84},{24,88},{28,92},{32,9... | collective-permute-start | bytes 196616 | tf_op jit(solution)/shard_map/ppermute | solution.py:18
  30.3 12.1 %collective-permute-start.2 = (f32[128,128]{0,1:T(8,128)S(1)}, f32[128,128]{0,1:T(8,128)S(1)}, u32[]{:S(2)}, u32[]{:S(2)}) collective-permute-start(f32[128,128]{0,1:T(8,128)S(1)} %get-tuple-element.36), channel_id=1, source_target_pairs={{0,128},{4,132},{8,136},{12,140},{16,144},{20,148},{24,152},{28,15... | collective-permute-start | bytes 196616 | tf_op jit(solution)/shard_map/ppermute | solution.py:18
  35.1 8.3 %collective-permute-start.1 = (f32[128,128]{0,1:T(8,128)S(1)}, f32[128,128]{0,1:T(8,128)S(1)}, u32[]{:S(2)}, u32[]{:S(2)}) collective-permute-start(f32[128,128]{0,1:T(8,128)S(1)} %get-tuple-element.37), channel_id=1, source_target_pairs={{0,192},{4,196},{8,200},{12,204},{16,208},{20,212},{24,216},{28,22... | collective-permute-start | bytes 196616 | tf_op jit(solution)/shard_map/ppermute | solution.py:18
  53.8 0.7 copy-start.1
  55.2 24.4 %copy-start.11 = (s32[128]{0:T(128)S(1)}, s32[128]{0:T(128)}, u32[]{:S(2)}) copy-start(s32[128]{0:T(128)} %param.7) | copy-start | bytes 1540
  55.8 34.2 %copy-start.10 = (bf16[512,5]{0,1:T(8,128)(2,1)S(1)}, bf16[512,5]{0,1:T(8,128)(2,1)}, u32[]{:S(2)}) copy-start(bf16[512,5]{0,1:T(8,128)(2,1)} %param.11) | copy-start | bytes 15364
  55.8 15.8 %collective-permute-start.8 = (f32[128,128]{0,1:T(8,128)S(1)}, f32[128,128]{0,1:T(8,128)S(1)}, u32[]{:S(2)}, u32[]{:S(2)}) collective-permute-start(f32[128,128]{0,1:T(8,128)S(1)} %get-tuple-element.24), channel_id=1, source_target_pairs={{0,384},{4,388},{8,392},{12,396},{16,400},{20,404},{24,408},{28,41... | collective-permute-start | bytes 196616 | tf_op jit(solution)/shard_map/ppermute | solution.py:18
  62.9 16.7 %collective-permute-start.13 = (f32[128,128]{0,1:T(8,128)S(1)}, f32[128,128]{0,1:T(8,128)S(1)}, u32[]{:S(2)}, u32[]{:S(2)}) collective-permute-start(f32[128,128]{0,1:T(8,128)S(1)} %get-tuple-element.25), channel_id=1, source_target_pairs={{384,0},{388,4},{392,8},{396,12},{400,16},{404,20},{408,24},{412,2... | collective-permute-start | bytes 196616 | tf_op jit(solution)/shard_map/ppermute | solution.py:18
  64.2 15.5 %collective-permute-start.12 = (f32[128,128]{0,1:T(8,128)S(1)}, f32[128,128]{0,1:T(8,128)S(1)}, u32[]{:S(2)}, u32[]{:S(2)}) collective-permute-start(f32[128,128]{0,1:T(8,128)S(1)} %get-tuple-element.26), channel_id=1, source_target_pairs={{256,0},{260,4},{264,8},{268,12},{272,16},{276,20},{280,24},{284,2... | collective-permute-start | bytes 196616 | tf_op jit(solution)/shard_map/ppermute | solution.py:18
  65.5 14.2 %collective-permute-start.11 = (f32[128,128]{0,1:T(8,128)S(1)}, f32[128,128]{0,1:T(8,128)S(1)}, u32[]{:S(2)}, u32[]{:S(2)}) collective-permute-start(f32[128,128]{0,1:T(8,128)S(1)} %get-tuple-element.27), channel_id=1, source_target_pairs={{128,0},{132,4},{136,8},{140,12},{144,16},{148,20},{152,24},{156,2... | collective-permute-start | bytes 196616 | tf_op jit(solution)/shard_map/ppermute | solution.py:18
  66.8 12.9 %collective-permute-start.10 = (f32[128,128]{0,1:T(8,128)S(1)}, f32[128,128]{0,1:T(8,128)S(1)}, u32[]{:S(2)}, u32[]{:S(2)}) collective-permute-start(f32[128,128]{0,1:T(8,128)S(1)} %get-tuple-element.28), channel_id=1, source_target_pairs={{0,128},{4,132},{8,136},{12,140},{16,144},{20,148},{24,152},{28,15... | collective-permute-start | bytes 196616 | tf_op jit(solution)/shard_map/ppermute | solution.py:18
  71.7 9.2 %collective-permute-start.9 = (f32[128,128]{0,1:T(8,128)S(1)}, f32[128,128]{0,1:T(8,128)S(1)}, u32[]{:S(2)}, u32[]{:S(2)}) collective-permute-start(f32[128,128]{0,1:T(8,128)S(1)} %get-tuple-element.29), channel_id=1, source_target_pairs={{0,256},{4,260},{8,264},{12,268},{16,272},{20,276},{24,280},{28,28... | collective-permute-start | bytes 196616 | tf_op jit(solution)/shard_map/ppermute | solution.py:18
  90.8 24.0 %copy-start.3 = (f32[128,512]{0,1:T(8,128)}, f32[128,512]{0,1:T(8,128)S(1)}, u32[]{:S(2)}) copy-start(f32[128,512]{0,1:T(8,128)S(1)} %copy.62) | copy-start | bytes 786436
  90.9 14.0 %collective-permute-start.14 = (bf16[128,128]{0,1:T(8,128)(2,1)S(1)}, bf16[128,128]{0,1:T(8,128)(2,1)S(1)}, u32[]{:S(2)}, u32[]{:S(2)}) collective-permute-start(bf16[128,128]{0,1:T(8,128)(2,1)S(1)} %fusion.19), channel_id=1, source_target_pairs={{384,0},{388,4},{392,8},{396,12},{400,16},{404,20},{408,24},{412,2... | collective-permute-start | bytes 98312 | tf_op jit(solution)/shard_map/ppermute | solution.py:18
  92.2 21.4 %collective-permute-start.19 = (bf16[128,128]{0,1:T(8,128)(2,1)S(1)}, bf16[128,128]{0,1:T(8,128)(2,1)S(1)}, u32[]{:S(2)}, u32[]{:S(2)}) collective-permute-start(bf16[128,128]{0,1:T(8,128)(2,1)S(1)} %fusion.19), channel_id=1, source_target_pairs={{0,384},{4,388},{8,392},{12,396},{16,400},{20,404},{24,408},{28,41... | collective-permute-start | bytes 98312 | tf_op jit(solution)/shard_map/ppermute | solution.py:18
  98.3 15.2 %collective-permute-start.18 = (bf16[128,128]{0,1:T(8,128)(2,1)S(1)}, bf16[128,128]{0,1:T(8,128)(2,1)S(1)}, u32[]{:S(2)}, u32[]{:S(2)}) collective-permute-start(bf16[128,128]{0,1:T(8,128)(2,1)S(1)} %fusion.19), channel_id=1, source_target_pairs={{0,256},{4,260},{8,264},{12,268},{16,272},{20,276},{24,280},{28,28... | collective-permute-start | bytes 98312 | tf_op jit(solution)/shard_map/ppermute | solution.py:18
  100.2 13.4 %collective-permute-start.17 = (bf16[128,128]{0,1:T(8,128)(2,1)S(1)}, bf16[128,128]{0,1:T(8,128)(2,1)S(1)}, u32[]{:S(2)}, u32[]{:S(2)}) collective-permute-start(bf16[128,128]{0,1:T(8,128)(2,1)S(1)} %fusion.19), channel_id=1, source_target_pairs={{0,128},{4,132},{8,136},{12,140},{16,144},{20,148},{24,152},{28,15... | collective-permute-start | bytes 98312 | tf_op jit(solution)/shard_map/ppermute | solution.py:18
  103.6 9.9 %collective-permute-start.16 = (bf16[128,128]{0,1:T(8,128)(2,1)S(1)}, bf16[128,128]{0,1:T(8,128)(2,1)S(1)}, u32[]{:S(2)}, u32[]{:S(2)}) collective-permute-start(bf16[128,128]{0,1:T(8,128)(2,1)S(1)} %fusion.19), channel_id=1, source_target_pairs={{128,0},{132,4},{136,8},{140,12},{144,16},{148,20},{152,24},{156,2... | collective-permute-start | bytes 98312 | tf_op jit(solution)/shard_map/ppermute | solution.py:18
  104.9 8.6 %collective-permute-start.15 = (bf16[128,128]{0,1:T(8,128)(2,1)S(1)}, bf16[128,128]{0,1:T(8,128)(2,1)S(1)}, u32[]{:S(2)}, u32[]{:S(2)}) collective-permute-start(bf16[128,128]{0,1:T(8,128)(2,1)S(1)} %fusion.19), channel_id=1, source_target_pairs={{256,0},{260,4},{264,8},{268,12},{272,16},{276,20},{280,24},{284,2... | collective-permute-start | bytes 98312 | tf_op jit(solution)/shard_map/ppermute | solution.py:18
  117.5 50.6 %copy-start.2 = (bf16[128,512]{0,1:T(8,128)(2,1)S(1)}, bf16[128,512]{0,1:T(8,128)(2,1)}, u32[]{:S(2)}) copy-start(bf16[128,512]{0,1:T(8,128)(2,1)} %copy-done.1) | copy-start | bytes 393220
  117.5 50.6 %copy-start.4 = (f32[128,512]{0,1:T(8,128)S(1)}, f32[128,512]{0,1:T(8,128)}, u32[]{:S(2)}) copy-start(f32[128,512]{0,1:T(8,128)} %copy-done.3) | copy-start | bytes 786436
  117.5 52.3 %copy-start.9 = (f32[128,128]{0,1:T(8,128)S(1)}, f32[128,128]{0,1:T(8,128)}, u32[]{:S(2)}) copy-start(f32[128,128]{0,1:T(8,128)} %get-tuple-element.23) | copy-start | bytes 196612
  117.5 94.2 %all-to-all-start.1 = ((bf16[9,128,4,128]{3,2,0,1:T(4,128)(2,1)}), bf16[9,128,4,128]{3,2,0,1:T(4,128)(2,1)S(1)}, u32[]{:S(2)}, u32[]{:S(2)}) async-start(bf16[9,128,4,128]{3,2,0,1:T(4,128)(2,1)} %copy.69), calls=%async_computation.1 | async-start | bytes 2359296 | tf_op jit(solution)/shard_map/all_to_all | solution.py:118
  130.5 76.6 %copy-start.8 = (bf16[128,512]{1,0:T(8,128)(2,1)S(1)}, bf16[128,512]{1,0:T(8,128)(2,1)}, u32[]{:S(2)}) copy-start(bf16[128,512]{1,0:T(8,128)(2,1)} %param.6) | copy-start | bytes 393220
  169.0 0.7 copy-start.5
  170.7 18.7 %collective-permute-start.20 = (bf16[128,128]{0,1:T(8,128)(2,1)S(1)}, bf16[128,128]{0,1:T(8,128)(2,1)S(1)}, u32[]{:S(2)}, u32[]{:S(2)}) collective-permute-start(bf16[128,128]{0,1:T(8,128)(2,1)S(1)} %fusion.24), channel_id=1, source_target_pairs={{256,0},{260,4},{264,8},{268,12},{272,16},{276,20},{280,24},{284,2... | collective-permute-start | bytes 98312 | tf_op jit(solution)/shard_map/ppermute | solution.py:18
  172.0 34.4 %collective-permute-start.27 = (bf16[128,128]{0,1:T(8,128)(2,1)S(1)}, bf16[128,128]{0,1:T(8,128)(2,1)S(1)}, u32[]{:S(2)}, u32[]{:S(2)}) collective-permute-start(bf16[128,128]{0,1:T(8,128)(2,1)S(1)} %fusion.24), channel_id=1, source_target_pairs={{0,256},{4,260},{8,264},{12,268},{16,272},{20,276},{24,280},{28,28... | collective-permute-start | bytes 98312 | tf_op jit(solution)/shard_map/ppermute | solution.py:18
  179.9 26.4 %collective-permute-start.26 = (bf16[128,128]{0,1:T(8,128)(2,1)S(1)}, bf16[128,128]{0,1:T(8,128)(2,1)S(1)}, u32[]{:S(2)}, u32[]{:S(2)}) collective-permute-start(bf16[128,128]{0,1:T(8,128)(2,1)S(1)} %fusion.24), channel_id=1, source_target_pairs={{0,192},{4,196},{8,200},{12,204},{16,208},{20,212},{24,216},{28,22... | collective-permute-start | bytes 98312 | tf_op jit(solution)/shard_map/ppermute | solution.py:18
  185.2 21.0 %collective-permute-start.25 = (bf16[128,128]{0,1:T(8,128)(2,1)S(1)}, bf16[128,128]{0,1:T(8,128)(2,1)S(1)}, u32[]{:S(2)}, u32[]{:S(2)}) collective-permute-start(bf16[128,128]{0,1:T(8,128)(2,1)S(1)} %fusion.24), channel_id=1, source_target_pairs={{0,128},{4,132},{8,136},{12,140},{16,144},{20,148},{24,152},{28,15... | collective-permute-start | bytes 98312 | tf_op jit(solution)/shard_map/ppermute | solution.py:18
  186.5 19.7 %collective-permute-start.24 = (bf16[128,128]{0,1:T(8,128)(2,1)S(1)}, bf16[128,128]{0,1:T(8,128)(2,1)S(1)}, u32[]{:S(2)}, u32[]{:S(2)}) collective-permute-start(bf16[128,128]{0,1:T(8,128)(2,1)S(1)} %fusion.24), channel_id=1, source_target_pairs={{0,64},{4,68},{8,72},{12,76},{16,80},{20,84},{24,88},{28,92},{32,9... | collective-permute-start | bytes 98312 | tf_op jit(solution)/shard_map/ppermute | solution.py:18
  189.4 6.5 %collective-permute-start.21 = (bf16[128,128]{0,1:T(8,128)(2,1)S(1)}, bf16[128,128]{0,1:T(8,128)(2,1)S(1)}, u32[]{:S(2)}, u32[]{:S(2)}) collective-permute-start(bf16[128,128]{0,1:T(8,128)(2,1)S(1)} %fusion.24), channel_id=1, source_target_pairs={{192,0},{196,4},{200,8},{204,12},{208,16},{212,20},{216,24},{220,2... | collective-permute-start | bytes 98312 | tf_op jit(solution)/shard_map/ppermute | solution.py:18
  195.8 5.5 %collective-permute-start.22 = (bf16[128,128]{0,1:T(8,128)(2,1)S(1)}, bf16[128,128]{0,1:T(8,128)(2,1)S(1)}, u32[]{:S(2)}, u32[]{:S(2)}) collective-permute-start(bf16[128,128]{0,1:T(8,128)(2,1)S(1)} %fusion.24), channel_id=1, source_target_pairs={{128,0},{132,4},{136,8},{140,12},{144,16},{148,20},{152,24},{156,2... | collective-permute-start | bytes 98312 | tf_op jit(solution)/shard_map/ppermute | solution.py:18
  201.4 4.9 %collective-permute-start.23 = (bf16[128,128]{0,1:T(8,128)(2,1)S(1)}, bf16[128,128]{0,1:T(8,128)(2,1)S(1)}, u32[]{:S(2)}, u32[]{:S(2)}) collective-permute-start(bf16[128,128]{0,1:T(8,128)(2,1)S(1)} %fusion.24), channel_id=1, source_target_pairs={{64,0},{68,4},{72,8},{76,12},{80,16},{84,20},{88,24},{92,28},{96,3... | collective-permute-start | bytes 98312 | tf_op jit(solution)/shard_map/ppermute | solution.py:18
  206.4 0.7 copy-start.6
  211.6 75.2 %all-to-all-start = ((bf16[9,128,4,128]{3,2,0,1:T(4,128)(2,1)}), bf16[9,128,4,128]{3,2,0,1:T(4,128)(2,1)S(1)}, u32[]{:S(2)}, u32[]{:S(2)}) async-start(bf16[9,128,4,128]{3,2,0,1:T(4,128)(2,1)} %copy.66), calls=%async_computation | async-start | bytes 2359296 | tf_op jit(solution)/shard_map/all_to_all | solution.py:118
  223.0 59.4 %all-reduce.5.cloned.1.call-start = ((), (), s32[]{:S(2)}) async-start(), calls=%async_computation.3 | async-start | bytes 262144 | tf_op jit(solution)/shard_map/psum | solution.py:113
Sparse Core Ops, SparseCore 0:
  114.9 53.0 all-reduce.2
  227.6 54.7 all-reduce.4
where the time goes:
time: 296 us; the launch traced here: 295 us
  starting transfers between devices  118 us (40%)
  waiting for transfers between devices  117 us (40%)
  blocking collectives  18.6 us (6%)
  between operations  14.7 us (5%)
  local copies, waits for them, and re-layouts  9.34 us (3%)
  matrix products  8.57 us (3%)
  other arithmetic  7.87 us (3%)
    psum x2, waiting for transfers between devices, block_backward_pass(): lax.psum(input_part.astype(jnp.bfloat16), 'mp').astype(jnp.float32)  94.4 us
    ppermute x28, starting transfers between devices, shifted(): return lax.ppermute(x, axis, pairs)  93.8 us
    all_to_all x2, starting transfers between devices, block_backward_pass(): lax.all_to_all(by_owner.astype(jnp.bfloat16), 'seq', split_axis=1, concat...  24.4 us
    ppermute x28, waiting for transfers between devices, shifted(): return lax.ppermute(x, axis, pairs)  23 us
    all_gather x2, blocking collectives, block_forward_pass(): lax.all_gather(activation.astype(jnp.bfloat16), 'mp', axis=1, tiled=True)  18.6 us
  transfers between devices with their start and end apart: 32, of which 9 were waited for; matrix products, arithmetic and copies ran while one was open for 6% of the time, Pallas kernels for 0%

commit v1 on v0

v1 whole, which is shorter than its diff:
```python
import functools
import itertools

import jax
import jax.numpy as jnp
from jax import lax
from jax.experimental import pallas as pl
from jax.experimental.pallas import tpu as pltpu
from jax.sharding import PartitionSpec as P

MESH = pl.DeviceIdType.MESH
ZN, XN, YN, MN = 8, 2, 8, 4
ROWS, CH, OWN, TAPS, VOCAB = 128, 512, 128, 9, 5
RES = ROWS // ZN
MID = TAPS // 2
HOP1, HOP2 = 1, 2
REACH1, REACH2 = 4, 3
HALO1, HALO2 = REACH1 * HOP1, REACH2 * HOP2
PIECE1, PIECE2 = 48, 32
AN, BN = 8, 16
SLICE = CH // AN
MODE = "cube"

epsilon = 1e-05
root_half = 0.7071067811865476
inv_root_two_pi = 0.3989422804014327


def nn(a, b):
    return lax.dot_general(a, b, (((1,), (0,)), ((), ())), preferred_element_type=jnp.float32)


def nt(a, b):
    return lax.dot_general(a, b, (((1,), (1,)), ((), ())), preferred_element_type=jnp.float32)


def split_dot(left, values):
    high = values.astype(jnp.bfloat16)
    low = (values - high.astype(jnp.float32)).astype(jnp.bfloat16)
    return nt(left, high) + nt(left, low)


def gelu_parts(conv_out):
    normal_cdf = 0.5 * (1.0 + lax.erf(conv_out * root_half))
    slope = normal_cdf + conv_out * inv_root_two_pi * jnp.exp(-0.5 * conv_out * conv_out)
    return conv_out * normal_cdf, slope


class Group:
    def __init__(self, coords, mods, place):
        self.coords, self.mods, self.place = coords, mods, place
        every = itertools.product(*(range(n) for n in mods))
        distance = lambda off: sum(min(o, n - o) for o, n in zip(off, mods))
        self.offsets = sorted((o for o in every if any(o)), key=lambda o: -distance(o))

    def moved(self, off, back):
        return tuple(
            c if o == 0 else lax.rem(c + (n - o if back else o), n)
            for c, o, n in zip(self.coords, off, self.mods)
        )

    def index(self, coords):
        at = coords[0]
        for c, n in zip(coords[1:], self.mods[1:]):
            at = at * n + c
        return at

    def me(self):
        return self.index(self.coords)

    def to(self, off):
        coords = self.moved(off, False)
        return self.index(coords), self.place(coords)

    def source(self, off):
        return self.index(self.moved(off, True))


def conv(x_ref, k_ref, hop, reach, acc_ref):
    acc_ref[...] = nn(x_ref[...], k_ref[MID])
    for j in range(-reach, reach + 1):
        if j == 0:
            continue
        n = (ZN - abs(j) * hop) * RES
        to = max(0, -j * hop) * RES
        at = max(0, j * hop) * RES
        acc_ref[to : to + n, :] += nn(x_ref[at : at + n, :], k_ref[MID + j])


def back_conv(d_ref, k_ref, hop, reach, acc_ref):
    acc_ref[...] = nt(d_ref[...], k_ref[MID])
    for j in range(-reach, reach + 1):
        if j == 0:
            continue
        n = (ZN - abs(j) * hop) * RES
        to = max(0, j * hop) * RES
        at = max(0, -j * hop) * RES
        acc_ref[to : to + n, :] += nt(d_ref[at : at + n, :], k_ref[MID + j])


def tap_gradients(ht_ref, d_ref, hop, reach, halo):
    left = ht_ref[...]
    out = []
    for j in range(-reach, reach + 1):
        at = halo - j * hop
        right = d_ref[:, at : at + ZN, :, :].reshape(AN * ROWS, OWN)
        out.append(nn(left, right))
    return out


def pieces(grads, send_ref):
    half = lax.broadcasted_iota(jnp.int32, (8, OWN), 0) < 4
    zero = jnp.zeros((8, OWN), jnp.float32)
    rows = send_ref.shape[1]
    for t in range(SLICE // 8):
        even, odd = [], []
        for p in range(rows // 8):
            a = grads[2 * p][8 * t : 8 * t + 8] if 2 * p < len(grads) else zero
            b = grads[2 * p + 1][8 * t : 8 * t + 8] if 2 * p + 1 < len(grads) else zero
            even.append(jnp.where(half, a, pltpu.roll(b, 4, 0)))
            odd.append(jnp.where(half, pltpu.roll(a, 4, 0), b))
        send_ref[2 * t] = jnp.concatenate(even, axis=0).astype(jnp.bfloat16)
        send_ref[2 * t + 1] = jnp.concatenate(odd, axis=0).astype(jnp.bfloat16)


def kernel(
    h_ref, ids_ref, mask_ref, k1_hbm, k2_hbm, w_ref,
    out_ref, dk1_ref, dk2_ref,
    k1, k2, x0, x1, tsend, tgot, perm, w8, acc, wide,
    act1, slope1, norm1, inv1, slope2, stat,
    hsend0, hsend1, ht0, ht1, d1, d2, dpad1, dpad2,
    psend1, psend2, pgot1, pgot2, rsend, rgot,
    gsend1, gsend2, ggot1, ggot2, zsend, zgot,
    send_sems, recv_sems, local_sems,
):
    f32, bf16 = jnp.float32, jnp.bfloat16
    s, m = lax.axis_index("seq"), lax.axis_index("mp")
    z = s // (XN * YN)
    xl = lax.rem(s // YN, XN)
    y = lax.rem(s, YN)
    seq_of = lambda z, x, y: (z * XN + x) * YN + y

    zs = Group((z,), (ZN,), lambda c: (seq_of(c[0], xl, y), m))
    ms = Group((m,), (MN,), lambda c: (s, c[0]))
    if MODE == "cube":
        z1, y1 = lax.rem(z, 2), lax.rem(y, 2)
        z2, y2 = z // 2, y // 2
        ga = Group((z1, xl, y1), (2, 2, 2), lambda c: (seq_of(z2 * 2 + c[0], c[1], y2 * 2 + c[2]), m))
        gb = Group((z2, y2), (4, 4), lambda c: (seq_of(c[0] * 2 + z1, xl, c[1] * 2 + y1), m))
        seq_at = lambda a, b: seq_of((b // 4) * 2 + a // 4, (a // 2) % 2, (b % 4) * 2 + a % 2)
    else:
        ga = Group((z,), (ZN,), lambda c: (seq_of(c[0], xl, y), m))
        gb = Group((xl, y), (XN, YN), lambda c: (seq_of(z, c[0], c[1]), m))
        seq_at = lambda a, b: a * BN + b

    count = itertools.count()
    started = []

    class Exchange:
        def __init__(self, group):
            self.group = group
            self.ids = {off: next(count) for off in group.offsets}

        def copy(self, off, src, dst, device):
            i = self.ids[off]
            return pltpu.make_async_remote_copy(
                src_ref=src, dst_ref=dst, send_sem=send_sems.at[i], recv_sem=recv_sems.at[i],
                device_id=device, device_id_type=MESH,
            )

        def start(self, src_of, dst_of):
            for off in self.group.offsets:
                to, device = self.group.to(off)
                copy = self.copy(off, src_of(to), dst_of(self.group.me()), device)
                copy.start()
                started.append(copy)

        def wait(self, dst_of):
            for off in self.group.offsets:
                at = dst_of(self.group.source(off))
                self.copy(off, at, at, self.group.to(off)[1]).wait_recv()

    rows16 = lambda i: pl.ds(pl.multiple_of(i * RES, RES), RES)
    lanes = lambda i: pl.ds(pl.multiple_of(i * 128, 128), 128)
    slices = lambda i: pl.ds(pl.multiple_of(i * SLICE, SLICE), SLICE)

    load_h = pltpu.make_async_copy(h_ref.at[rows16(z)], x0.at[rows16(z)], local_sems.at[0])
    load_k1 = pltpu.make_async_copy(k1_hbm, k1, local_sems.at[1])
    load_k2 = pltpu.make_async_copy(k2_hbm, k2, local_sems.at[2])
    load_h.start()
    load_k1.start()
    load_k2.start()

    barrier = pltpu.get_barrier_semaphore()
    seen = 0
    covered = {"cube": (ga, gb), "z": (gb,)}[MODE]
    for group in (zs, ms) + covered:
        for off in group.offsets:
            if MODE == "cube" and group is not zs and group is not ms:
                if not any(off[1:]):
                    continue
            pl.semaphore_signal(barrier, inc=1, device_id=group.to(off)[1], device_id_type=MESH)
            seen += 1

    lane = lax.broadcasted_iota(jnp.int32, (8, 128), 1)
    sub = lax.broadcasted_iota(jnp.int32, (8, 128), 0)
    position = lane + s * ROWS
    hit = position == mask_ref[0]
    for q in range(1, 16):
        hit = jnp.logical_or(hit, position == mask_ref[q])
    target = jnp.where(hit, jnp.broadcast_to(ids_ref[...], (8, 128)), -1).astype(f32)
    target = pltpu.roll(target, z * RES, 1)
    tsend[...] = target
    tgot[z] = target

    p = lax.broadcasted_iota(jnp.int32, (CH, CH), 0)
    a, b, low = p // SLICE, (p // 4) % BN, p % 4
    channel = seq_at(a, b) * 4 + low
    perm[...] = (lax.broadcasted_iota(jnp.int32, (CH, CH), 1) == channel).astype(f32).astype(bf16)

    wt = jnp.transpose(w_ref[...].astype(f32))
    w8[...] = jnp.concatenate([wt, jnp.zeros((8 - VOCAB, CH), f32)], axis=0)
    for dpad, halo in ((dpad1, HALO1), (dpad2, HALO2)):
        zero = jnp.zeros((AN, halo, RES, OWN), bf16)
        dpad[:, 0:halo] = zero
        dpad[:, halo + ZN : 2 * halo + ZN] = zero

    pl.semaphore_wait(barrier, seen)

    move_h = Exchange(zs)
    move_t = Exchange(zs)
    move_h.start(lambda to: h_ref.at[rows16(to)], lambda me: x0.at[rows16(me)])
    move_t.start(lambda to: tsend, lambda me: tgot.at[me])
    load_h.wait()
    load_k1.wait()
    move_h.wait(lambda frm: x0.at[rows16(frm)])

    conv(x0, k1, HOP1, REACH1, acc)
    activation, slope = gelu_parts(acc[...])
    slope1[...] = slope
    act1[m] = activation.astype(bf16)
    gather1 = Exchange(ms)
    gather1.start(lambda to: act1.at[m], lambda me: act1.at[me])

    mine = ga.me()
    hsend0[...] = nt(perm[...], x0[...]).astype(bf16)
    ht0[:, lanes(mine)] = hsend0[slices(mine), :]
    move_t.wait(lambda frm: tgot.at[frm])
    load_k2.wait()
    gather1.wait(lambda frm: act1.at[frm])
    move0 = Exchange(ga)
    move0.start(lambda to: hsend0.at[slices(to)], lambda me: ht0.at[:, lanes(me)])

    values = jnp.concatenate([act1[i] for i in range(MN)], axis=1).astype(f32)
    centred = values - jnp.mean(values, axis=1, keepdims=True)
    inverse = lax.rsqrt(jnp.mean(centred * centred, axis=1, keepdims=True) + epsilon)
    normed = centred * inverse
    for i in range(MN):
        norm1[i] = normed[:, i * 128 : i * 128 + 128]
    inv1[...] = jnp.broadcast_to(inverse, (ROWS, 128))
    x1[...] = (x0[...].astype(f32) + normed).astype(bf16)

    conv(x1, k2, HOP2, REACH2, acc)
    activation, slope = gelu_parts(acc[...])
    slope2[...] = slope
    act2 = activation.astype(bf16)
    values2 = act2.astype(f32)
    w_own = w8[:, lanes(m)]
    sub_own = lax.broadcasted_iota(jnp.int32, (8, OWN), 0)
    left = jnp.where(sub_own == VOCAB, 1.0, w_own).astype(bf16)
    ones = jnp.ones((8, OWN), bf16)
    off_mean = values2 - jnp.mean(values2, axis=1, keepdims=True)
    sums = nt(left, act2)
    squares = split_dot(ones, off_mean * off_mean)
    stat[m] = jnp.where(sub == VOCAB + 1, squares, sums)
    share = Exchange(ms)
    share.start(lambda to: stat.at[m], lambda me: stat.at[me])

    hsend1[...] = nt(perm[...], x1[...]).astype(bf16)
    ht1[:, lanes(mine)] = hsend1[slices(mine), :]
    own_logits = nt(w8[...].astype(bf16), x1[...])
    w_sum = jnp.sum(w8[...], axis=1, keepdims=True)
    turned = pltpu.roll(tgot[:, 0, :], lax.rem(ROWS - z * RES, ROWS), 1)
    targets = jnp.sum(jnp.where(lane // RES == sub, turned, 0.0), axis=0, keepdims=True)
    share.wait(lambda frm: stat.at[frm])

    each = [stat[i] for i in range(MN)]
    total = each[0] + each[1] + each[2] + each[3]
    mean2 = total[VOCAB : VOCAB + 1] * (1.0 / CH)
    spread = total[VOCAB + 1 : VOCAB + 2]
    for part in each:
        apart = part[VOCAB : VOCAB + 1] * (1.0 / OWN) - mean2
        spread = spread + OWN * apart * apart
    inv2 = lax.rsqrt(spread * (1.0 / CH) + epsilon)
    along = inv2 * (total - mean2 * w_sum)
    logits = own_logits + along
    classes = sub < VOCAB
    exponent = jnp.where(classes, jnp.exp(logits), 0.0)
    probability = exponent / jnp.sum(exponent, axis=0, keepdims=True)
    onehot = (sub.astype(f32) == targets).astype(f32)
    dlogits = jnp.where(jnp.logical_and(classes, targets >= 0.0), probability - onehot, 0.0)
    mean_grad = jnp.sum(dlogits * w_sum, axis=0, keepdims=True) * (1.0 / CH)
    mean_cross = jnp.sum(jnp.where(classes, dlogits * along, 0.0), axis=0, keepdims=True) * (1.0 / CH)
    slant = inv2 * mean_cross
    shift = mean_grad - slant * mean2
    packed = jnp.where(sub == 5, inv2, jnp.where(sub == 6, shift, jnp.where(sub == 7, slant, dlogits)))
    by_row = jnp.transpose(jnp.concatenate([packed, jnp.zeros((ROWS - 8, 128), f32)], axis=0))
    grad2 = by_row[:, 0:1] * w_own[0:1]
    for v in range(1, VOCAB):
        grad2 = grad2 + by_row[:, v : v + 1] * w_own[v : v + 1]
    dconv = by_row[:, 5:6] * (grad2 - by_row[:, 6:7] - values2 * by_row[:, 7:8]) * slope2[...]
    dconv = dconv.astype(bf16)
    d2[...] = dconv
    dpad2[mine, HALO2 : HALO2 + ZN] = dconv.reshape(ZN, RES, OWN)

    back_conv(d2, k2, HOP2, REACH2, wide)
    first = grad2
    second = grad2 * norm1[m]
    for i in range(MN):
        part = wide[:, i * 128 : i * 128 + 128].astype(bf16)
        psend2[i] = part
        part = part.astype(f32)
        first = first + part
        second = second + part * norm1[i]
    pgot2[m] = psend2[m]
    reduce2 = Exchange(ms)
    reduce2.start(lambda to: psend2.at[to], lambda me: pgot2.at[me])
    rows_sum = jnp.where(sub == 0, split_dot(ones, first), split_dot(ones, second))
    rsend[...] = rows_sum
    rgot[m] = rows_sum
    reduce_rows = Exchange(ms)
    reduce_rows.start(lambda to: rsend, lambda me: rgot.at[me])

    move1 = Exchange(ga)
    move1.start(lambda to: hsend1.at[slices(to)], lambda me: ht1.at[:, lanes(me)])
    share2 = Exchange(ga)
    share2.start(lambda to: dpad2.at[mine, pl.ds(HALO2, ZN)], lambda me: dpad2.at[me, pl.ds(HALO2, ZN)])

    reduce2.wait(lambda frm: pgot2.at[frm])
    reduce_rows.wait(lambda frm: rgot.at[frm])
    grad1 = grad2
    for i in range(MN):
        grad1 = grad1 + pgot2[i].astype(f32)
    rows_sum = (rgot[0] + rgot[1] + rgot[2] + rgot[3]) * (1.0 / CH)
    by_row = jnp.transpose(jnp.concatenate([rows_sum, jnp.zeros((ROWS - 8, 128), f32)], axis=0))
    dconv = inv1[...] * (grad1 - by_row[:, 0:1] - norm1[m] * by_row[:, 1:2]) * slope1[...]
    dconv = dconv.astype(bf16)
    d1[...] = dconv
    dpad1[mine, HALO1 : HALO1 + ZN] = dconv.reshape(ZN, RES, OWN)
    share1 = Exchange(ga)
    share1.start(lambda to: dpad1.at[mine, pl.ds(HALO1, ZN)], lambda me: dpad1.at[me, pl.ds(HALO1, ZN)])

    back_conv(d1, k1, HOP1, REACH1, wide)
    for i in range(MN):
        psend1[i] = wide[:, i * 128 : i * 128 + 128].astype(bf16)
    pgot1[m] = psend1[m]
    reduce1 = Exchange(ms)
    reduce1.start(lambda to: psend1.at[to], lambda me: pgot1.at[me])

    move1.wait(lambda frm: ht1.at[:, lanes(frm)])
    share2.wait(lambda frm: dpad2.at[frm, pl.ds(HALO2, ZN)])
    owner = gb.me()
    pieces(tap_gradients(ht1, dpad2, HOP2, REACH2, HALO2), gsend2)
    ggot2[owner] = gsend2[owner]
    scatter2 = Exchange(gb)
    scatter2.start(lambda to: gsend2.at[to], lambda me: ggot2.at[me])

    reduce1.wait(lambda frm: pgot1.at[frm])
    for i in range(MN):
        grad1 = grad1 + pgot1[i].astype(f32)
    zsend[...] = grad1.astype(bf16)
    zgot[rows16(z), :] = zsend[rows16(z), :]
    move_back = Exchange(zs)
    move_back.start(lambda to: zsend.at[rows16(to)], lambda me: zgot.at[rows16(me)])

    move0.wait(lambda frm: ht0.at[:, lanes(frm)])
    share1.wait(lambda frm: dpad1.at[frm, pl.ds(HALO1, ZN)])
    pieces(tap_gradients(ht0, dpad1, HOP1, REACH1, HALO1), gsend1)
    ggot1[owner] = gsend1[owner]
    scatter1 = Exchange(gb)
    scatter1.start(lambda to: gsend1.at[to], lambda me: ggot1.at[me])

    move_back.wait(lambda frm: zgot.at[rows16(frm)])
    keep = pltpu.make_async_copy(zgot, out_ref.at[:, lanes(m)], local_sems.at[3])
    keep.start()
    gather_out = Exchange(ms)
    gather_out.start(lambda to: zgot, lambda me: out_ref.at[:, lanes(me)])

    scatter2.wait(lambda frm: ggot2.at[frm])
    grads = ggot2[0].astype(f32)
    for i in range(1, BN):
        grads = grads + ggot2[i].astype(f32)
    dk2_ref[...] = jnp.zeros((TAPS, 4, OWN), f32)
    for j in range(2 * REACH2 + 1):
        dk2_ref[MID - REACH2 + j] = grads[4 * j : 4 * j + 4]

    scatter1.wait(lambda frm: ggot1.at[frm])
    grads = ggot1[0].astype(f32)
    for i in range(1, BN):
        grads = grads + ggot1[i].astype(f32)
    for j in range(TAPS):
        dk1_ref[j] = grads[4 * j : 4 * j + 4]

    gather_out.wait(lambda frm: out_ref.at[:, lanes(frm)])
    keep.wait()
    for copy in started:
        copy.wait_send()


def local(h, ids, mask_index, k1, k2, w):
    f32, bf16 = jnp.float32, jnp.bfloat16
    vmem = pltpu.VMEM
    hbm = pl.BlockSpec(memory_space=pltpu.HBM)
    inside = pl.BlockSpec(memory_space=pltpu.VMEM)
    copies = 8 * 7 + 6 * 3 + 2 * 15 + 8
    return pl.pallas_call(
        kernel,
        out_shape=(
            jax.ShapeDtypeStruct((ROWS, CH), bf16),
            jax.ShapeDtypeStruct((TAPS, 4, OWN), f32),
            jax.ShapeDtypeStruct((TAPS, 4, OWN), f32),
        ),
        in_specs=[hbm, inside, pl.BlockSpec(memory_space=pltpu.SMEM), hbm, hbm, inside],
        out_specs=(hbm, inside, inside),
        scratch_shapes=[
            vmem((TAPS, CH, OWN), bf16),
            vmem((TAPS, CH, OWN), bf16),
            vmem((ROWS, CH), bf16),
            vmem((ROWS, CH), bf16),
            vmem((8, 128), f32),
            vmem((ZN, 8, 128), f32),
            vmem((CH, CH), bf16),
            vmem((8, CH), f32),
            vmem((ROWS, OWN), f32),
            vmem((ROWS, CH), f32),
            vmem((MN, ROWS, OWN), bf16),
            vmem((ROWS, OWN), f32),
            vmem((MN, ROWS, OWN), f32),
            vmem((ROWS, 128), f32),
            vmem((ROWS, OWN), f32),
            vmem((MN, 8, 128), f32),
            vmem((CH, ROWS), bf16),
            vmem((CH, ROWS), bf16),
            vmem((SLICE, AN * ROWS), bf16),
            vmem((SLICE, AN * ROWS), bf16),
            vmem((ROWS, OWN), bf16),
            vmem((ROWS, OWN), bf16),
            vmem((AN, ZN + 2 * HALO1, RES, OWN), bf16),
            vmem((AN, ZN + 2 * HALO2, RES, OWN), bf16),
            vmem((MN, ROWS, OWN), bf16),
            vmem((MN, ROWS, OWN), bf16),
            vmem((MN, ROWS, OWN), bf16),
            vmem((MN, ROWS, OWN), bf16),
            vmem((8, 128), f32),
            vmem((MN, 8, 128), f32),
            vmem((BN, PIECE1, OWN), bf16),
            vmem((BN, PIECE2, OWN), bf16),
            vmem((BN, PIECE1, OWN), bf16),
            vmem((BN, PIECE2, OWN), bf16),
            vmem((ROWS, OWN), bf16),
            vmem((ROWS, OWN), bf16),
            pltpu.SemaphoreType.DMA((copies,)),
            pltpu.SemaphoreType.DMA((copies,)),
            pltpu.SemaphoreType.DMA((4,)),
        ],
        compiler_params=pltpu.CompilerParams(
            collective_id=0, has_side_effects=True, vmem_limit_bytes=40 * 1024 * 1024
        ),
    )(h, ids.reshape(1, ROWS), mask_index, k1, k2, w)


def solution(mesh):
    placed = (P("seq", None), P("seq"), P("seq"), P(None, None, "mp"), P(None, None, "mp"), P())
    return jax.shard_map(
        local,
        mesh=mesh,
        in_specs=placed,
        out_specs=(P("seq", None), P(None, "seq", "mp"), P(None, "seq", "mp")),
        check_vma=False,
    )
```

time: 296 us -> 68.6 us (0.23)
  starting transfers between devices: 118 us -> 0 us
  waiting for transfers between devices: 117 us -> 0 us
  Pallas kernels: 0 us -> 60.2 us
  blocking collectives: 18.6 us -> 0 us
  between operations: 14.7 us -> 0.66 us
  matrix products: 8.57 us -> 0 us
  other arithmetic: 7.87 us -> 0 us
    psum x2 -> x0, waiting for transfers between devices: 94.4 us -> none  [block_backward_pass(): lax.psum(input_part.astype(jnp.bfloat16), 'mp').astype(jnp.float32)]
    ppermute x28 -> x0, starting transfers between devices: 93.8 us -> none  [shifted(): return lax.ppermute(x, axis, pairs)]
    pallas_call x0 -> x1, Pallas kernels: none -> 60.2 us  [local(): pl.pallas_call(kernel, out_shape=(jax.ShapeDtypeStruct((ROWS, CH), bf16),...]
    all_to_all x2 -> x0, starting transfers between devices: 24.4 us -> none  [block_backward_pass(): lax.all_to_all(by_owner.astype(jnp.bfloat16), 'seq', split_axis=1, concat...]
    ppermute x28 -> x0, waiting for transfers between devices: 23 us -> none  [shifted(): return lax.ppermute(x, axis, pairs)]
    all_gather x2 -> x0, blocking collectives: 18.6 us -> none  [block_forward_pass(): lax.all_gather(activation.astype(jnp.bfloat16), 'mp', axis=1, tiled=True)]
    dot_general x8 -> x0, matrix products: 8.57 us -> none  [the longest x2 3.59 us: block_backward_pass(): jnp.einsum('kro,kdo->rd', tap_stack, kernel, preferred_element_type=jnp.f...]
    convert_element_type x4 -> x0, local copies, waits for them, and re-layouts: 5.27 us -> none  [block_backward_pass(): by_owner.astype(jnp.bfloat16)]
  transfers between devices with their start and end apart: 32 -> 0, of which waited for: 9 -> 0; matrix products, arithmetic and copies ran while one was open for 6% -> 0% of each run, Pallas kernels for 0% -> 0%
where the time goes in v1:
time: 68.6 us; the launch traced here: 68.4 us
  Pallas kernels  60.2 us (88%)
  local copies, waits for them, and re-layouts  7.49 us (11%)
    pallas_call x1, Pallas kernels, local(): pl.pallas_call(kernel, out_shape=(jax.ShapeDtypeStruct((ROWS, CH), bf16),...  60.2 us
    unnamed x14, local copies, waits for them, and re-layouts  7.49 us

profile of v1, /device:TPU:1, one launch (start us, length us, event | category | flops | bytes accessed | tf_op | source)
XLA Modules:
  0.0 68.4 jit_solution(3344815342696899808)
XLA Ops:
  0.6 0.9 %copy.9.w_ref = bf16[512,5]{1,0:T(8,128)(2,1)S(1)} copy(bf16[512,5]{0,1:T(8,128)(2,1)} %param.11) | data formatting | bytes 10240 | tf_op args[5]
  1.5 0.0 copy-start
  1.5 1.3 %copy-done = bf16[9,512,128]{2,1,0:T(8,128)(2,1)S(1)} copy-done((bf16[9,512,128]{2,1,0:T(8,128)(2,1)S(1)}, bf16[9,512,128]{2,1,0:T(8,128)(2,1)}, u32[]{:S(2)}) %copy-start) | copy-done | bytes 1179672
  2.8 0.0 copy-start.1
  2.8 1.3 %copy-done.1 = bf16[9,512,128]{2,1,0:T(8,128)(2,1)S(1)} copy-done((bf16[9,512,128]{2,1,0:T(8,128)(2,1)S(1)}, bf16[9,512,128]{2,1,0:T(8,128)(2,1)}, u32[]{:S(2)}) %copy-start.1) | copy-done | bytes 1179672
  4.1 0.0 copy-start.2
  4.1 0.9 %copy-done.2 = bf16[128,512]{1,0:T(8,128)(2,1)S(1)} copy-done((bf16[128,512]{1,0:T(8,128)(2,1)S(1)}, bf16[128,512]{1,0:T(8,128)(2,1)}, u32[]{:S(2)}) %copy-start.2) | copy-done | bytes 131096
  5.0 0.0 copy-start.3
  5.0 0.7 copy-done.3
  5.6 0.0 copy-start.4
  5.6 0.7 copy-done.4
  6.3 60.2 %shard_map.85 = (bf16[128,512]{1,0:T(8,128)(2,1)S(1)}, f32[9,4,128]{2,1,0:T(4,128)S(1)}, f32[9,4,128]{2,1,0:T(4,128)S(1)}) custom-call(bf16[128,512]{1,0:T(8,128)(2,1)S(1)} %copy-done.2, s32[1,128]{1,0:T(1,128)S(1)} %bitcast.1, s32[16]{0:T(128)S(1)} %copy-done.4, bf16[9,512,128]{2,1,0:T(8,128)(2,1)S(1)} %copy-done, bf16[9,512,128]{2,1,0:T(8,128)(2,1)S(1)} %copy-done.1, ...), custom_call_target="tpu_custom_call" | custom-call | tf_op jit(solution)/shard_map/pallas_call | solution.py:416
  66.5 0.7 copy.13
  67.1 0.6 copy.14
  67.8 0.6 copy.15
Async XLA Ops:
  1.5 1.3 %copy-start = (bf16[9,512,128]{2,1,0:T(8,128)(2,1)S(1)}, bf16[9,512,128]{2,1,0:T(8,128)(2,1)}, u32[]{:S(2)}) copy-start(bf16[9,512,128]{2,1,0:T(8,128)(2,1)} %k1_hbm.1) | copy-start | bytes 3538948
  2.8 1.3 %copy-start.1 = (bf16[9,512,128]{2,1,0:T(8,128)(2,1)S(1)}, bf16[9,512,128]{2,1,0:T(8,128)(2,1)}, u32[]{:S(2)}) copy-start(bf16[9,512,128]{2,1,0:T(8,128)(2,1)} %k2_hbm.1) | copy-start | bytes 3538948
  4.1 0.9 %copy-start.2 = (bf16[128,512]{1,0:T(8,128)(2,1)S(1)}, bf16[128,512]{1,0:T(8,128)(2,1)}, u32[]{:S(2)}) copy-start(bf16[128,512]{1,0:T(8,128)(2,1)} %h_ref.1) | copy-start | bytes 393220
  5.0 0.7 copy-start.3
  5.6 0.7 copy-start.4

commit v2 on v1

--- a/solution.py
+++ b/solution.py
@@ -124,9 +124,9 @@
 
 
 def kernel(
-    h_ref, ids_ref, mask_ref, k1_hbm, k2_hbm, w_ref,
-    out_ref, dk1_ref, dk2_ref,
-    k1, k2, x0, x1, tsend, tgot, perm, w8, acc, wide,
+    h_ref, ids_hbm, mask_hbm, k1_hbm, k2_hbm, w_hbm,
+    out_ref, dk1_hbm, dk2_hbm,
+    ids_ref, mask_ref, w_ref, dk1_ref, dk2_ref, k1, k2, hv, x0, x1, tsend, tgot, perm, w8, acc, wide,
     act1, slope1, norm1, inv1, slope2, stat,
     hsend0, hsend1, ht0, ht1, d1, d2, dpad1, dpad2,
     psend1, psend2, pgot1, pgot2, rsend, rgot,
@@ -147,7 +147,7 @@
         z2, y2 = z // 2, y // 2
         ga = Group((z1, xl, y1), (2, 2, 2), lambda c: (seq_of(z2 * 2 + c[0], c[1], y2 * 2 + c[2]), m))
         gb = Group((z2, y2), (4, 4), lambda c: (seq_of(c[0] * 2 + z1, xl, c[1] * 2 + y1), m))
-        seq_at = lambda a, b: seq_of((b // 4) * 2 + a // 4, (a // 2) % 2, (b % 4) * 2 + a % 2)
+        seq_at = lambda a, b: seq_of((b >> 2) * 2 + (a >> 2), (a >> 1) & 1, (b & 3) * 2 + (a & 1))
     else:
         ga = Group((z,), (ZN,), lambda c: (seq_of(c[0], xl, y), m))
         gb = Group((xl, y), (XN, YN), lambda c: (seq_of(z, c[0], c[1]), m))
@@ -157,39 +157,31 @@
     started = []
 
     class Exchange:
-        def __init__(self, group):
-            self.group = group
-            self.ids = {off: next(count) for off in group.offsets}
-
-        def copy(self, off, src, dst, device):
-            i = self.ids[off]
+        def __init__(self, group, bytes_of_all):
+            self.group, self.i = group, next(count)
+            self.all = self.copy(bytes_of_all, bytes_of_all, group.to(group.offsets[0])[1])
+
+        def copy(self, src, dst, device):
             return pltpu.make_async_remote_copy(
-                src_ref=src, dst_ref=dst, send_sem=send_sems.at[i], recv_sem=recv_sems.at[i],
+                src_ref=src, dst_ref=dst, send_sem=send_sems.at[self.i], recv_sem=recv_sems.at[self.i],
                 device_id=device, device_id_type=MESH,
             )
 
         def start(self, src_of, dst_of):
             for off in self.group.offsets:
                 to, device = self.group.to(off)
-                copy = self.copy(off, src_of(to), dst_of(self.group.me()), device)
-                copy.start()
-                started.append(copy)
-
-        def wait(self, dst_of):
-            for off in self.group.offsets:
-                at = dst_of(self.group.source(off))
-                self.copy(off, at, at, self.group.to(off)[1]).wait_recv()
+                self.copy(src_of(to), dst_of(self.group.me()), device).start()
+            started.append(self)
+
+        def wait(self):
+            self.all.wait_recv()
+
+        def wait_send(self):
+            self.all.wait_send()
 
     rows16 = lambda i: pl.ds(pl.multiple_of(i * RES, RES), RES)
     lanes = lambda i: pl.ds(pl.multiple_of(i * 128, 128), 128)
     slices = lambda i: pl.ds(pl.multiple_of(i * SLICE, SLICE), SLICE)
-
-    load_h = pltpu.make_async_copy(h_ref.at[rows16(z)], x0.at[rows16(z)], local_sems.at[0])
-    load_k1 = pltpu.make_async_copy(k1_hbm, k1, local_sems.at[1])
-    load_k2 = pltpu.make_async_copy(k2_hbm, k2, local_sems.at[2])
-    load_h.start()
-    load_k1.start()
-    load_k2.start()
 
     barrier = pltpu.get_barrier_semaphore()
     seen = 0
@@ -202,6 +194,28 @@
             pl.semaphore_signal(barrier, inc=1, device_id=group.to(off)[1], device_id_type=MESH)
             seen += 1
 
+    load_h = pltpu.make_async_copy(h_ref, hv, local_sems.at[0])
+    load_k1 = pltpu.make_async_copy(k1_hbm, k1, local_sems.at[1])
+    load_k2 = pltpu.make_async_copy(k2_hbm, k2, local_sems.at[2])
+    load_ids = pltpu.make_async_copy(ids_hbm, ids_ref, local_sems.at[4])
+    load_mask = pltpu.make_async_copy(mask_hbm, mask_ref, local_sems.at[5])
+    load_w = pltpu.make_async_copy(w_hbm, w_ref, local_sems.at[6])
+    load_h.start()
+    load_k1.start()
+    load_ids.start()
+    load_mask.start()
+    load_w.start()
+    load_k2.start()
+
+    load_h.wait()
+    pl.semaphore_wait(barrier, seen)
+
+    move_h = Exchange(zs, x0.at[pl.ds(0, ROWS - RES)])
+    move_h.start(lambda to: hv.at[rows16(to)], lambda me: x0.at[rows16(me)])
+    x0[rows16(z), :] = hv[rows16(z), :]
+
+    load_ids.wait()
+    load_mask.wait()
     lane = lax.broadcasted_iota(jnp.int32, (8, 128), 1)
     sub = lax.broadcasted_iota(jnp.int32, (8, 128), 0)
     position = lane + s * ROWS
@@ -211,45 +225,42 @@
     target = jnp.where(hit, jnp.broadcast_to(ids_ref[...], (8, 128)), -1).astype(f32)
     target = pltpu.roll(target, z * RES, 1)
     tsend[...] = target
-    tgot[z] = target
-
-    p = lax.broadcasted_iota(jnp.int32, (CH, CH), 0)
-    a, b, low = p // SLICE, (p // 4) % BN, p % 4
-    channel = seq_at(a, b) * 4 + low
-    perm[...] = (lax.broadcasted_iota(jnp.int32, (CH, CH), 1) == channel).astype(f32).astype(bf16)
-
-    wt = jnp.transpose(w_ref[...].astype(f32))
-    w8[...] = jnp.concatenate([wt, jnp.zeros((8 - VOCAB, CH), f32)], axis=0)
+    row = lambda i: pl.ds(i, 1)
+    move_t = Exchange(zs, tgot.at[pl.ds(0, ZN - 1)])
+    move_t.start(lambda to: tsend.at[row(0)], lambda me: tgot.at[row(me)])
+    tgot[row(z), :] = target[0:1]
+
+    p = lax.broadcasted_iota(jnp.int32, (CH, 128), 0)
+    a, b, low = p >> 6, (p >> 2) & (BN - 1), p & 3
+    channel = seq_at(a, b) * 4 + low - lax.broadcasted_iota(jnp.int32, (CH, 128), 1)
+    for i in range(CH // 128):
+        perm[:, i * 128 : i * 128 + 128] = (channel == i * 128).astype(f32).astype(bf16)
+
+    load_w.wait()
+    w8[...] = jnp.concatenate([w_ref[...].astype(f32), jnp.zeros((8 - VOCAB, CH), f32)], axis=0)
     for dpad, halo in ((dpad1, HALO1), (dpad2, HALO2)):
         zero = jnp.zeros((AN, halo, RES, OWN), bf16)
         dpad[:, 0:halo] = zero
         dpad[:, halo + ZN : 2 * halo + ZN] = zero
 
-    pl.semaphore_wait(barrier, seen)
-
-    move_h = Exchange(zs)
-    move_t = Exchange(zs)
-    move_h.start(lambda to: h_ref.at[rows16(to)], lambda me: x0.at[rows16(me)])
-    move_t.start(lambda to: tsend, lambda me: tgot.at[me])
-    load_h.wait()
     load_k1.wait()
-    move_h.wait(lambda frm: x0.at[rows16(frm)])
+    move_h.wait()
 
     conv(x0, k1, HOP1, REACH1, acc)
     activation, slope = gelu_parts(acc[...])
     slope1[...] = slope
     act1[m] = activation.astype(bf16)
-    gather1 = Exchange(ms)
+    gather1 = Exchange(ms, act1.at[pl.ds(0, MN - 1)])
     gather1.start(lambda to: act1.at[m], lambda me: act1.at[me])
 
     mine = ga.me()
     hsend0[...] = nt(perm[...], x0[...]).astype(bf16)
     ht0[:, lanes(mine)] = hsend0[slices(mine), :]
-    move_t.wait(lambda frm: tgot.at[frm])
+    move0 = Exchange(ga, ht0.at[:, pl.ds(0, (AN - 1) * ROWS)])
+    move0.start(lambda to: hsend0.at[slices(to)], lambda me: ht0.at[:, lanes(me)])
+    move_t.wait()
     load_k2.wait()
-    gather1.wait(lambda frm: act1.at[frm])
-    move0 = Exchange(ga)
-    move0.start(lambda to: hsend0.at[slices(to)], lambda me: ht0.at[:, lanes(me)])
+    gather1.wait()
 
     values = jnp.concatenate([act1[i] for i in range(MN)], axis=1).astype(f32)
     centred = values - jnp.mean(values, axis=1, keepdims=True)
@@ -273,16 +284,18 @@
     sums = nt(left, act2)
     squares = split_dot(ones, off_mean * off_mean)
     stat[m] = jnp.where(sub == VOCAB + 1, squares, sums)
-    share = Exchange(ms)
+    share = Exchange(ms, stat.at[pl.ds(0, MN - 1)])
     share.start(lambda to: stat.at[m], lambda me: stat.at[me])
 
     hsend1[...] = nt(perm[...], x1[...]).astype(bf16)
     ht1[:, lanes(mine)] = hsend1[slices(mine), :]
+    move1 = Exchange(ga, ht1.at[:, pl.ds(0, (AN - 1) * ROWS)])
+    move1.start(lambda to: hsend1.at[slices(to)], lambda me: ht1.at[:, lanes(me)])
     own_logits = nt(w8[...].astype(bf16), x1[...])
     w_sum = jnp.sum(w8[...], axis=1, keepdims=True)
-    turned = pltpu.roll(tgot[:, 0, :], lax.rem(ROWS - z * RES, ROWS), 1)
+    turned = pltpu.roll(tgot[...], lax.rem(ROWS - z * RES, ROWS), 1)
     targets = jnp.sum(jnp.where(lane // RES == sub, turned, 0.0), axis=0, keepdims=True)
-    share.wait(lambda frm: stat.at[frm])
+    share.wait()
 
     each = [stat[i] for i in range(MN)]
     total = each[0] + each[1] + each[2] + each[3]
@@ -313,6 +326,9 @@
     d2[...] = dconv
     dpad2[mine, HALO2 : HALO2 + ZN] = dconv.reshape(ZN, RES, OWN)
 
+    share2 = Exchange(ga, dpad2.at[pl.ds(0, AN - 1), pl.ds(HALO2, ZN)])
+    share2.start(lambda to: dpad2.at[mine, pl.ds(HALO2, ZN)], lambda me: dpad2.at[me, pl.ds(HALO2, ZN)])
+
     back_conv(d2, k2, HOP2, REACH2, wide)
     first = grad2
     second = grad2 * norm1[m]
@@ -323,21 +339,16 @@
         first = first + part
         second = second + part * norm1[i]
     pgot2[m] = psend2[m]
-    reduce2 = Exchange(ms)
+    reduce2 = Exchange(ms, pgot2.at[pl.ds(0, MN - 1)])
     reduce2.start(lambda to: psend2.at[to], lambda me: pgot2.at[me])
     rows_sum = jnp.where(sub == 0, split_dot(ones, first), split_dot(ones, second))
     rsend[...] = rows_sum
     rgot[m] = rows_sum
-    reduce_rows = Exchange(ms)
+    reduce_rows = Exchange(ms, rgot.at[pl.ds(0, MN - 1)])
     reduce_rows.start(lambda to: rsend, lambda me: rgot.at[me])
 
-    move1 = Exchange(ga)
-    move1.start(lambda to: hsend1.at[slices(to)], lambda me: ht1.at[:, lanes(me)])
-    share2 = Exchange(ga)
-    share2.start(lambda to: dpad2.at[mine, pl.ds(HALO2, ZN)], lambda me: dpad2.at[me, pl.ds(HALO2, ZN)])
-
-    reduce2.wait(lambda frm: pgot2.at[frm])
-    reduce_rows.wait(lambda frm: rgot.at[frm])
+    reduce2.wait()
+    reduce_rows.wait()
     grad1 = grad2
     for i in range(MN):
         grad1 = grad1 + pgot2[i].astype(f32)
@@ -347,72 +358,77 @@
     dconv = dconv.astype(bf16)
     d1[...] = dconv
     dpad1[mine, HALO1 : HALO1 + ZN] = dconv.reshape(ZN, RES, OWN)
-    share1 = Exchange(ga)
+    share1 = Exchange(ga, dpad1.at[pl.ds(0, AN - 1), pl.ds(HALO1, ZN)])
     share1.start(lambda to: dpad1.at[mine, pl.ds(HALO1, ZN)], lambda me: dpad1.at[me, pl.ds(HALO1, ZN)])
 
     back_conv(d1, k1, HOP1, REACH1, wide)
     for i in range(MN):
         psend1[i] = wide[:, i * 128 : i * 128 + 128].astype(bf16)
     pgot1[m] = psend1[m]
-    reduce1 = Exchange(ms)
+    reduce1 = Exchange(ms, pgot1.at[pl.ds(0, MN - 1)])
     reduce1.start(lambda to: psend1.at[to], lambda me: pgot1.at[me])
 
-    move1.wait(lambda frm: ht1.at[:, lanes(frm)])
-    share2.wait(lambda frm: dpad2.at[frm, pl.ds(HALO2, ZN)])
+    move1.wait()
+    share2.wait()
     owner = gb.me()
     pieces(tap_gradients(ht1, dpad2, HOP2, REACH2, HALO2), gsend2)
     ggot2[owner] = gsend2[owner]
-    scatter2 = Exchange(gb)
+    scatter2 = Exchange(gb, ggot2.at[pl.ds(0, BN - 1)])
     scatter2.start(lambda to: gsend2.at[to], lambda me: ggot2.at[me])
 
-    reduce1.wait(lambda frm: pgot1.at[frm])
+    reduce1.wait()
     for i in range(MN):
         grad1 = grad1 + pgot1[i].astype(f32)
     zsend[...] = grad1.astype(bf16)
     zgot[rows16(z), :] = zsend[rows16(z), :]
-    move_back = Exchange(zs)
+    move_back = Exchange(zs, zgot.at[pl.ds(0, ROWS - RES)])
     move_back.start(lambda to: zsend.at[rows16(to)], lambda me: zgot.at[rows16(me)])
 
-    move0.wait(lambda frm: ht0.at[:, lanes(frm)])
-    share1.wait(lambda frm: dpad1.at[frm, pl.ds(HALO1, ZN)])
+    move0.wait()
+    share1.wait()
     pieces(tap_gradients(ht0, dpad1, HOP1, REACH1, HALO1), gsend1)
     ggot1[owner] = gsend1[owner]
-    scatter1 = Exchange(gb)
+    scatter1 = Exchange(gb, ggot1.at[pl.ds(0, BN - 1)])
     scatter1.start(lambda to: gsend1.at[to], lambda me: ggot1.at[me])
 
-    move_back.wait(lambda frm: zgot.at[rows16(frm)])
+    move_back.wait()
     keep = pltpu.make_async_copy(zgot, out_ref.at[:, lanes(m)], local_sems.at[3])
     keep.start()
-    gather_out = Exchange(ms)
+    gather_out = Exchange(ms, out_ref.at[:, pl.ds(0, CH - OWN)])
     gather_out.start(lambda to: zgot, lambda me: out_ref.at[:, lanes(me)])
 
-    scatter2.wait(lambda frm: ggot2.at[frm])
+    scatter2.wait()
     grads = ggot2[0].astype(f32)
     for i in range(1, BN):
         grads = grads + ggot2[i].astype(f32)
     dk2_ref[...] = jnp.zeros((TAPS, 4, OWN), f32)
     for j in range(2 * REACH2 + 1):
         dk2_ref[MID - REACH2 + j] = grads[4 * j : 4 * j + 4]
-
-    scatter1.wait(lambda frm: ggot1.at[frm])
+    store2 = pltpu.make_async_copy(dk2_ref, dk2_hbm, local_sems.at[7])
+    store2.start()
+
+    scatter1.wait()
     grads = ggot1[0].astype(f32)
     for i in range(1, BN):
         grads = grads + ggot1[i].astype(f32)
     for j in range(TAPS):
         dk1_ref[j] = grads[4 * j : 4 * j + 4]
-
-    gather_out.wait(lambda frm: out_ref.at[:, lanes(frm)])
+    store1 = pltpu.make_async_copy(dk1_ref, dk1_hbm, local_sems.at[8])
+    store1.start()
+
+    gather_out.wait()
     keep.wait()
-    for copy in started:
-        copy.wait_send()
+    store2.wait()
+    store1.wait()
+    for exchange in started:
+        exchange.wait_send()
 
 
 def local(h, ids, mask_index, k1, k2, w):
     f32, bf16 = jnp.float32, jnp.bfloat16
     vmem = pltpu.VMEM
     hbm = pl.BlockSpec(memory_space=pltpu.HBM)
-    inside = pl.BlockSpec(memory_space=pltpu.VMEM)
-    copies = 8 * 7 + 6 * 3 + 2 * 15 + 8
+    copies = 15
     return pl.pallas_call(
         kernel,
         out_shape=(
@@ -420,15 +436,21 @@
             jax.ShapeDtypeStruct((TAPS, 4, OWN), f32),
             jax.ShapeDtypeStruct((TAPS, 4, OWN), f32),
         ),
-        in_specs=[hbm, inside, pl.BlockSpec(memory_space=pltpu.SMEM), hbm, hbm, inside],
-        out_specs=(hbm, inside, inside),
+        in_specs=[hbm] * 6,
+        out_specs=(hbm, hbm, hbm),
         scratch_shapes=[
+            vmem((1, ROWS), jnp.int32),
+            pltpu.SMEM((16,), jnp.int32),
+            vmem((VOCAB, CH), bf16),
+            vmem((TAPS, 4, OWN), f32),
+            vmem((TAPS, 4, OWN), f32),
             vmem((TAPS, CH, OWN), bf16),
             vmem((TAPS, CH, OWN), bf16),
             vmem((ROWS, CH), bf16),
             vmem((ROWS, CH), bf16),
+            vmem((ROWS, CH), bf16),
             vmem((8, 128), f32),
-            vmem((ZN, 8, 128), f32),
+            vmem((ZN, 128), f32),
             vmem((CH, CH), bf16),
             vmem((8, CH), f32),
             vmem((ROWS, OWN), f32),
@@ -461,12 +483,12 @@
             vmem((ROWS, OWN), bf16),
             pltpu.SemaphoreType.DMA((copies,)),
             pltpu.SemaphoreType.DMA((copies,)),
-            pltpu.SemaphoreType.DMA((4,)),
+            pltpu.SemaphoreType.DMA((9,)),
         ],
         compiler_params=pltpu.CompilerParams(
-            collective_id=0, has_side_effects=True, vmem_limit_bytes=40 * 1024 * 1024
+            collective_id=0, has_side_effects=True, vmem_limit_bytes=60 * 1024 * 1024
         ),
-    )(h, ids.reshape(1, ROWS), mask_index, k1, k2, w)
+    )(h, ids.reshape(1, ROWS), mask_index, k1, k2, w.T)
 
 
 def solution(mesh):

time: 68.6 us -> 61.5 us (0.90)
  Pallas kernels: 60.2 us -> 56.3 us
  local copies, waits for them, and re-layouts: 7.49 us -> 4.23 us
    pallas_call x1, Pallas kernels: 60.2 us -> 56.3 us  [local(): pl.pallas_call(kernel, out_shape=(jax.ShapeDtypeStruct((ROWS, CH), bf16),...]
    unnamed x14 -> x3, local copies, waits for them, and re-layouts: 7.49 us -> 4.23 us
where the time goes in v2:
time: 61.5 us; the launch traced here: 61.2 us
  Pallas kernels  56.3 us (92%)
  local copies, waits for them, and re-layouts  4.23 us (7%)
  between operations  0.64 us (1%)
    pallas_call x1, Pallas kernels, local(): pl.pallas_call(kernel, out_shape=(jax.ShapeDtypeStruct((ROWS, CH), bf16),...  56.3 us
    unnamed x3, local copies, waits for them, and re-layouts  4.23 us

profile of v2, /device:TPU:1, one launch (start us, length us, event | category | flops | bytes accessed | tf_op | source)
XLA Modules:
  0.0 61.2 jit_solution(14789339531807410545)
XLA Ops:
  0.6 56.3 %shard_map.85 = (bf16[128,512]{1,0:T(8,128)(2,1)}, f32[9,4,128]{2,1,0:T(4,128)}, f32[9,4,128]{2,1,0:T(4,128)}) custom-call(bf16[128,512]{1,0:T(8,128)(2,1)} %h_ref.1, s32[1,128]{1,0:T(1,128)} %bitcast.3, s32[16]{0:T(128)} %mask_hbm.1, bf16[9,512,128]{2,1,0:T(8,128)(2,1)} %k1_hbm.1, bf16[9,512,128]{2,1,0:T(8,128)(2,1)} %k2_hbm.1, bf16[5,512]{1,0:T(8,128)(2,1)} %bitcast.2), custom_call_target="tpu_custom_call" | custom-call | tf_op jit(solution)/shard_map/pallas_call | solution.py:432
  57.0 1.6 %copy.12 = bf16[128,512]{1,0:T(8,128)(2,1)} copy(bf16[128,512]{1,0:T(8,128)(2,1)} %get-tuple-element.6) | data formatting | bytes 262144
  58.5 1.3 %copy.13 = f32[9,4,128]{2,1,0:T(4,128)} copy(f32[9,4,128]{2,1,0:T(4,128)} %get-tuple-element.7) | data formatting | bytes 36864
  59.9 1.3 %copy.14 = f32[9,4,128]{2,1,0:T(4,128)} copy(f32[9,4,128]{2,1,0:T(4,128)} %get-tuple-element.8) | data formatting | bytes 36864

commit v3 on v2

--- a/solution.py
+++ b/solution.py
@@ -130,8 +130,8 @@
     act1, slope1, norm1, inv1, slope2, stat,
     hsend0, hsend1, ht0, ht1, d1, d2, dpad1, dpad2,
     psend1, psend2, pgot1, pgot2, rsend, rgot,
-    gsend1, gsend2, ggot1, ggot2, zsend, zgot,
-    send_sems, recv_sems, local_sems,
+    gsend1, gsend2, ggot1, ggot2, zsend, zgot, final,
+    send_sems, recv_sems, local_sems, ready_y, ready_x,
 ):
     f32, bf16 = jnp.float32, jnp.bfloat16
     s, m = lax.axis_index("seq"), lax.axis_index("mp")
@@ -142,6 +142,11 @@
 
     zs = Group((z,), (ZN,), lambda c: (seq_of(c[0], xl, y), m))
     ms = Group((m,), (MN,), lambda c: (s, c[0]))
+    ys = Group((y,), (YN,), lambda c: (seq_of(z, xl, c[0]), m))
+    xs = Group((xl,), (XN,), lambda c: (seq_of(z, c[0], y), m))
+    core, xh = lax.rem(m, 2), m // 2
+    cs = Group((core,), (2,), lambda c: (s, xh * 2 + c[0]))
+    zx = Group((z, xh), (ZN, 2), lambda c: (seq_of(c[0], xl, y), c[1] * 2 + core))
     if MODE == "cube":
         z1, y1 = lax.rem(z, 2), lax.rem(y, 2)
         z2, y2 = z // 2, y // 2
@@ -171,7 +176,8 @@
             for off in self.group.offsets:
                 to, device = self.group.to(off)
                 self.copy(src_of(to), dst_of(self.group.me()), device).start()
-            started.append(self)
+            if self not in started:
+                started.append(self)
 
         def wait(self):
             self.all.wait_recv()
@@ -185,12 +191,8 @@
 
     barrier = pltpu.get_barrier_semaphore()
     seen = 0
-    covered = {"cube": (ga, gb), "z": (gb,)}[MODE]
-    for group in (zs, ms) + covered:
+    for group in (zs, ys, ms, xs):
         for off in group.offsets:
-            if MODE == "cube" and group is not zs and group is not ms:
-                if not any(off[1:]):
-                    continue
             pl.semaphore_signal(barrier, inc=1, device_id=group.to(off)[1], device_id_type=MESH)
             seen += 1
 
@@ -213,6 +215,8 @@
     move_h = Exchange(zs, x0.at[pl.ds(0, ROWS - RES)])
     move_h.start(lambda to: hv.at[rows16(to)], lambda me: x0.at[rows16(me)])
     x0[rows16(z), :] = hv[rows16(z), :]
+    for off in ys.offsets:
+        pl.semaphore_signal(ready_y, inc=1, device_id=ys.to(off)[1], device_id_type=MESH)
 
     load_ids.wait()
     load_mask.wait()
@@ -253,9 +257,13 @@
     gather1 = Exchange(ms, act1.at[pl.ds(0, MN - 1)])
     gather1.start(lambda to: act1.at[m], lambda me: act1.at[me])
 
+    pl.semaphore_wait(ready_y, YN - 1)
+    pl.semaphore_signal(ready_x, inc=1, device_id=xs.to((1,))[1], device_id_type=MESH)
+
     mine = ga.me()
     hsend0[...] = nt(perm[...], x0[...]).astype(bf16)
     ht0[:, lanes(mine)] = hsend0[slices(mine), :]
+    pl.semaphore_wait(ready_x, XN - 1)
     move0 = Exchange(ga, ht0.at[:, pl.ds(0, (AN - 1) * ROWS)])
     move0.start(lambda to: hsend0.at[slices(to)], lambda me: ht0.at[:, lanes(me)])
     move_t.wait()
@@ -326,9 +334,6 @@
     d2[...] = dconv
     dpad2[mine, HALO2 : HALO2 + ZN] = dconv.reshape(ZN, RES, OWN)
 
-    share2 = Exchange(ga, dpad2.at[pl.ds(0, AN - 1), pl.ds(HALO2, ZN)])
-    share2.start(lambda to: dpad2.at[mine, pl.ds(HALO2, ZN)], lambda me: dpad2.at[me, pl.ds(HALO2, ZN)])
-
     back_conv(d2, k2, HOP2, REACH2, wide)
     first = grad2
     second = grad2 * norm1[m]
@@ -347,6 +352,8 @@
     reduce_rows = Exchange(ms, rgot.at[pl.ds(0, MN - 1)])
     reduce_rows.start(lambda to: rsend, lambda me: rgot.at[me])
 
+    share2 = Exchange(ga, dpad2.at[pl.ds(0, AN - 1), pl.ds(HALO2, ZN)])
+    share2.start(lambda to: dpad2.at[mine, pl.ds(HALO2, ZN)], lambda me: dpad2.at[me, pl.ds(HALO2, ZN)])
     reduce2.wait()
     reduce_rows.wait()
     grad1 = grad2
@@ -362,11 +369,13 @@
     share1.start(lambda to: dpad1.at[mine, pl.ds(HALO1, ZN)], lambda me: dpad1.at[me, pl.ds(HALO1, ZN)])
 
     back_conv(d1, k1, HOP1, REACH1, wide)
-    for i in range(MN):
-        psend1[i] = wide[:, i * 128 : i * 128 + 128].astype(bf16)
-    pgot1[m] = psend1[m]
-    reduce1 = Exchange(ms, pgot1.at[pl.ds(0, MN - 1)])
-    reduce1.start(lambda to: psend1.at[to], lambda me: pgot1.at[me])
+    for c in range(2):
+        for i in range(2):
+            at = (i * 2 + c) * 128
+            psend1[c, i] = wide[:, at : at + 128].astype(bf16)
+    reduce1 = Exchange(cs, pgot1)
+    reduce1.start(lambda to: psend1.at[to], lambda me: pgot1)
+    wide[:, lanes(m)] += grad1
 
     move1.wait()
     share2.wait()
@@ -377,12 +386,11 @@
     scatter2.start(lambda to: gsend2.at[to], lambda me: ggot2.at[me])
 
     reduce1.wait()
-    for i in range(MN):
-        grad1 = grad1 + pgot1[i].astype(f32)
-    zsend[...] = grad1.astype(bf16)
-    zgot[rows16(z), :] = zsend[rows16(z), :]
-    move_back = Exchange(zs, zgot.at[pl.ds(0, ROWS - RES)])
-    move_back.start(lambda to: zsend.at[rows16(to)], lambda me: zgot.at[rows16(me)])
+    for i in range(2):
+        zsend[i] = (wide[:, lanes(i * 2 + core)] + pgot1[i].astype(f32)).astype(bf16)
+    zgot[zx.me()] = zsend[:, rows16(z), :]
+    move_back = Exchange(zx, zgot.at[pl.ds(0, 2 * ZN - 1)])
+    move_back.start(lambda to: zsend.at[:, rows16(to // 2)], lambda me: zgot.at[me])
 
     move0.wait()
     share1.wait()
@@ -392,10 +400,16 @@
     scatter1.start(lambda to: gsend1.at[to], lambda me: ggot1.at[me])
 
     move_back.wait()
-    keep = pltpu.make_async_copy(zgot, out_ref.at[:, lanes(m)], local_sems.at[3])
-    keep.start()
-    gather_out = Exchange(ms, out_ref.at[:, pl.ds(0, CH - OWN)])
-    gather_out.start(lambda to: zgot, lambda me: out_ref.at[:, lanes(me)])
+    gather_out = Exchange(cs, out_ref.at[:, pl.ds(0, 2 * OWN)])
+    keep = []
+    for i in range(2):
+        for r in range(ZN):
+            total = zgot[2 * r, i].astype(f32) + zgot[2 * r + 1, i].astype(f32)
+            final[i, r * RES : r * RES + RES] = total.astype(bf16)
+        place = out_ref.at[:, lanes(i * 2 + core)]
+        keep.append(pltpu.make_async_copy(final.at[i], place, local_sems.at[3 + 6 * i]))
+        keep[i].start()
+        gather_out.start(lambda to: final.at[i], lambda me: place)
 
     scatter2.wait()
     grads = ggot2[0].astype(f32)
@@ -417,7 +431,8 @@
     store1.start()
 
     gather_out.wait()
-    keep.wait()
+    for copy in keep:
+        copy.wait()
     store2.wait()
     store1.wait()
     for exchange in started:
@@ -469,9 +484,9 @@
             vmem((ROWS, OWN), bf16),
             vmem((AN, ZN + 2 * HALO1, RES, OWN), bf16),
             vmem((AN, ZN + 2 * HALO2, RES, OWN), bf16),
+            vmem((2, 2, ROWS, OWN), bf16),
             vmem((MN, ROWS, OWN), bf16),
-            vmem((MN, ROWS, OWN), bf16),
-            vmem((MN, ROWS, OWN), bf16),
+            vmem((2, ROWS, OWN), bf16),
             vmem((MN, ROWS, OWN), bf16),
             vmem((8, 128), f32),
             vmem((MN, 8, 128), f32),
@@ -479,11 +494,14 @@
             vmem((BN, PIECE2, OWN), bf16),
             vmem((BN, PIECE1, OWN), bf16),
             vmem((BN, PIECE2, OWN), bf16),
-            vmem((ROWS, OWN), bf16),
-            vmem((ROWS, OWN), bf16),
+            vmem((2, ROWS, OWN), bf16),
+            vmem((2 * ZN, 2, RES, OWN), bf16),
+            vmem((2, ROWS, OWN), bf16),
             pltpu.SemaphoreType.DMA((copies,)),
             pltpu.SemaphoreType.DMA((copies,)),
-            pltpu.SemaphoreType.DMA((9,)),
+            pltpu.SemaphoreType.DMA((10,)),
+            pltpu.SemaphoreType.REGULAR,
+            pltpu.SemaphoreType.REGULAR,
         ],
         compiler_params=pltpu.CompilerParams(
             collective_id=0, has_side_effects=True, vmem_limit_bytes=60 * 1024 * 1024

time: 61.5 us -> 60 us (0.976); the launches traced: 61.2 us -> 59 us
  Pallas kernels: 56.3 us -> 54.1 us
    pallas_call x1, Pallas kernels: 56.3 us -> 54.1 us  [local(): pl.pallas_call(kernel, out_shape=(jax.ShapeDtypeStruct((ROWS, CH), bf16),...]
where the time goes in v3:
time: 60 us; the launch traced here: 59 us
  Pallas kernels  54.1 us (90%)
  local copies, waits for them, and re-layouts  4.23 us (7%)
  between operations  0.64 us (1%)
    pallas_call x1, Pallas kernels, local(): pl.pallas_call(kernel, out_shape=(jax.ShapeDtypeStruct((ROWS, CH), bf16),...  54.1 us
    unnamed x3, local copies, waits for them, and re-layouts  4.23 us

profile of v3, /device:TPU:1, one launch (start us, length us, event | category | flops | bytes accessed | tf_op | source)
XLA Modules:
  0.0 59.0 jit_solution(1041233797565400944)
XLA Ops:
  0.6 54.1 %shard_map.85 = (bf16[128,512]{1,0:T(8,128)(2,1)}, f32[9,4,128]{2,1,0:T(4,128)}, f32[9,4,128]{2,1,0:T(4,128)}) custom-call(bf16[128,512]{1,0:T(8,128)(2,1)} %h_ref.1, s32[1,128]{1,0:T(1,128)} %bitcast.3, s32[16]{0:T(128)} %mask_hbm.1, bf16[9,512,128]{2,1,0:T(8,128)(2,1)} %k1_hbm.1, bf16[9,512,128]{2,1,0:T(8,128)(2,1)} %k2_hbm.1, bf16[5,512]{1,0:T(8,128)(2,1)} %bitcast.2), custom_call_target="tpu_custom_call" | custom-call | tf_op jit(solution)/shard_map/pallas_call | solution.py:447
  54.8 1.6 %copy.12 = bf16[128,512]{1,0:T(8,128)(2,1)} copy(bf16[128,512]{1,0:T(8,128)(2,1)} %get-tuple-element.6) | data formatting | bytes 262144
  56.3 1.3 %copy.13 = f32[9,4,128]{2,1,0:T(4,128)} copy(f32[9,4,128]{2,1,0:T(4,128)} %get-tuple-element.7) | data formatting | bytes 36864
  57.7 1.3 %copy.14 = f32[9,4,128]{2,1,0:T(4,128)} copy(f32[9,4,128]{2,1,0:T(4,128)} %get-tuple-element.8) | data formatting | bytes 36864

commit v4 on v3

--- a/solution.py
+++ b/solution.py
@@ -16,7 +16,7 @@
 HOP1, HOP2 = 1, 2
 REACH1, REACH2 = 4, 3
 HALO1, HALO2 = REACH1 * HOP1, REACH2 * HOP2
-PIECE1, PIECE2 = 48, 32
+PIECE = 64
 AN, BN = 8, 16
 SLICE = CH // AN
 MODE = "cube"
@@ -98,6 +98,18 @@
         acc_ref[to : to + n, :] += nt(d_ref[at : at + n, :], k_ref[MID + j])
 
 
+def back_conv_part(d_ref, k_ref, hop, reach, part, acc_ref):
+    channels = pl.ds(pl.multiple_of(part * OWN, OWN), OWN)
+    acc_ref[...] = nt(d_ref[...], k_ref[MID, channels, :])
+    for j in range(-reach, reach + 1):
+        if j == 0:
+            continue
+        n = (ZN - abs(j) * hop) * RES
+        to = max(0, j * hop) * RES
+        at = max(0, -j * hop) * RES
+        acc_ref[to : to + n, :] += nt(d_ref[at : at + n, :], k_ref[MID + j, channels, :])
+
+
 def tap_gradients(ht_ref, d_ref, hop, reach, halo):
     left = ht_ref[...]
     out = []
@@ -108,19 +120,17 @@
     return out
 
 
-def pieces(grads, send_ref):
+def pieces(grads, send_ref, first):
     half = lax.broadcasted_iota(jnp.int32, (8, OWN), 0) < 4
-    zero = jnp.zeros((8, OWN), jnp.float32)
-    rows = send_ref.shape[1]
     for t in range(SLICE // 8):
         even, odd = [], []
-        for p in range(rows // 8):
-            a = grads[2 * p][8 * t : 8 * t + 8] if 2 * p < len(grads) else zero
-            b = grads[2 * p + 1][8 * t : 8 * t + 8] if 2 * p + 1 < len(grads) else zero
+        for a, b in zip(grads[::2], grads[1::2]):
+            a, b = a[8 * t : 8 * t + 8], b[8 * t : 8 * t + 8]
             even.append(jnp.where(half, a, pltpu.roll(b, 4, 0)))
             odd.append(jnp.where(half, pltpu.roll(a, 4, 0), b))
-        send_ref[2 * t] = jnp.concatenate(even, axis=0).astype(jnp.bfloat16)
-        send_ref[2 * t + 1] = jnp.concatenate(odd, axis=0).astype(jnp.bfloat16)
+        last = first + 8 * len(even)
+        send_ref[2 * t, first:last] = jnp.concatenate(even, axis=0).astype(jnp.bfloat16)
+        send_ref[2 * t + 1, first:last] = jnp.concatenate(odd, axis=0).astype(jnp.bfloat16)
 
 
 def kernel(
@@ -130,7 +140,7 @@
     act1, slope1, norm1, inv1, slope2, stat,
     hsend0, hsend1, ht0, ht1, d1, d2, dpad1, dpad2,
     psend1, psend2, pgot1, pgot2, rsend, rgot,
-    gsend1, gsend2, ggot1, ggot2, zsend, zgot, final,
+    gsend, ggot, rest2, zsend, zgot, final,
     send_sems, recv_sems, local_sems, ready_y, ready_x,
 ):
     f32, bf16 = jnp.float32, jnp.bfloat16
@@ -176,6 +186,11 @@
             for off in self.group.offsets:
                 to, device = self.group.to(off)
                 self.copy(src_of(to), dst_of(self.group.me()), device).start()
+            if self not in started:
+                started.append(self)
+
+        def start_one(self, off, src, dst):
+            self.copy(src, dst, self.group.to(off)[1]).start()
             if self not in started:
                 started.append(self)
 
@@ -334,26 +349,30 @@
     d2[...] = dconv
     dpad2[mine, HALO2 : HALO2 + ZN] = dconv.reshape(ZN, RES, OWN)
 
-    back_conv(d2, k2, HOP2, REACH2, wide)
+    share2 = Exchange(ga, dpad2.at[pl.ds(0, AN - 1), pl.ds(HALO2, ZN)])
+    share2.start(lambda to: dpad2.at[mine, pl.ds(HALO2, ZN)], lambda me: dpad2.at[me, pl.ds(HALO2, ZN)])
+
     first = grad2
     second = grad2 * norm1[m]
-    for i in range(MN):
-        part = wide[:, i * 128 : i * 128 + 128].astype(bf16)
-        psend2[i] = part
+    reduce2 = Exchange(ms, pgot2.at[pl.ds(0, MN - 1)])
+    for step in (2, 3, 1, 0):
+        i = lax.rem(m + step, MN)
+        back_conv_part(d2, k2, HOP2, REACH2, i, acc)
+        part = acc[...].astype(bf16)
+        if step:
+            psend2[i] = part
+            reduce2.start_one((step,), psend2.at[i], pgot2.at[m])
+        else:
+            pgot2[m] = part
         part = part.astype(f32)
         first = first + part
         second = second + part * norm1[i]
-    pgot2[m] = psend2[m]
-    reduce2 = Exchange(ms, pgot2.at[pl.ds(0, MN - 1)])
-    reduce2.start(lambda to: psend2.at[to], lambda me: pgot2.at[me])
     rows_sum = jnp.where(sub == 0, split_dot(ones, first), split_dot(ones, second))
     rsend[...] = rows_sum
     rgot[m] = rows_sum
     reduce_rows = Exchange(ms, rgot.at[pl.ds(0, MN - 1)])
     reduce_rows.start(lambda to: rsend, lambda me: rgot.at[me])
 
-    share2 = Exchange(ga, dpad2.at[pl.ds(0, AN - 1), pl.ds(HALO2, ZN)])
-    share2.start(lambda to: dpad2.at[mine, pl.ds(HALO2, ZN)], lambda me: dpad2.at[me, pl.ds(HALO2, ZN)])
     reduce2.wait()
     reduce_rows.wait()
     grad1 = grad2
@@ -380,10 +399,10 @@
     move1.wait()
     share2.wait()
     owner = gb.me()
-    pieces(tap_gradients(ht1, dpad2, HOP2, REACH2, HALO2), gsend2)
-    ggot2[owner] = gsend2[owner]
-    scatter2 = Exchange(gb, ggot2.at[pl.ds(0, BN - 1)])
-    scatter2.start(lambda to: gsend2.at[to], lambda me: ggot2.at[me])
+    grads = tap_gradients(ht1, dpad2, HOP2, REACH2, HALO2)
+    pieces(grads[:4], gsend, 0)
+    for i in range(3):
+        rest2[i] = grads[4 + i]
 
     reduce1.wait()
     for i in range(2):
@@ -394,10 +413,11 @@
 
     move0.wait()
     share1.wait()
-    pieces(tap_gradients(ht0, dpad1, HOP1, REACH1, HALO1), gsend1)
-    ggot1[owner] = gsend1[owner]
-    scatter1 = Exchange(gb, ggot1.at[pl.ds(0, BN - 1)])
-    scatter1.start(lambda to: gsend1.at[to], lambda me: ggot1.at[me])
+    grads = tap_gradients(ht0, dpad1, HOP1, REACH1, HALO1)
+    pieces([rest2[i] for i in range(3)] + grads, gsend, 16)
+    ggot[owner] = gsend[owner]
+    scatter = Exchange(gb, ggot.at[pl.ds(0, BN - 1)])
+    scatter.start(lambda to: gsend.at[to], lambda me: ggot.at[me])
 
     move_back.wait()
     gather_out = Exchange(cs, out_ref.at[:, pl.ds(0, 2 * OWN)])
@@ -411,23 +431,19 @@
         keep[i].start()
         gather_out.start(lambda to: final.at[i], lambda me: place)
 
-    scatter2.wait()
-    grads = ggot2[0].astype(f32)
+    dk2_ref[0] = jnp.zeros((4, OWN), f32)
+    dk2_ref[TAPS - 1] = jnp.zeros((4, OWN), f32)
+    scatter.wait()
+    grads = ggot[0].astype(f32)
     for i in range(1, BN):
-        grads = grads + ggot2[i].astype(f32)
-    dk2_ref[...] = jnp.zeros((TAPS, 4, OWN), f32)
+        grads = grads + ggot[i].astype(f32)
     for j in range(2 * REACH2 + 1):
         dk2_ref[MID - REACH2 + j] = grads[4 * j : 4 * j + 4]
+    for j in range(TAPS):
+        dk1_ref[j] = grads[28 + 4 * j : 32 + 4 * j]
     store2 = pltpu.make_async_copy(dk2_ref, dk2_hbm, local_sems.at[7])
+    store1 = pltpu.make_async_copy(dk1_ref, dk1_hbm, local_sems.at[8])
     store2.start()
-
-    scatter1.wait()
-    grads = ggot1[0].astype(f32)
-    for i in range(1, BN):
-        grads = grads + ggot1[i].astype(f32)
-    for j in range(TAPS):
-        dk1_ref[j] = grads[4 * j : 4 * j + 4]
-    store1 = pltpu.make_async_copy(dk1_ref, dk1_hbm, local_sems.at[8])
     store1.start()
 
     gather_out.wait()
@@ -444,6 +460,7 @@
     vmem = pltpu.VMEM
     hbm = pl.BlockSpec(memory_space=pltpu.HBM)
     copies = 15
+    operands = (h, ids.reshape(1, ROWS), mask_index, k1, k2, w.T)
     return pl.pallas_call(
         kernel,
         out_shape=(
@@ -490,10 +507,9 @@
             vmem((MN, ROWS, OWN), bf16),
             vmem((8, 128), f32),
             vmem((MN, 8, 128), f32),
-            vmem((BN, PIECE1, OWN), bf16),
-            vmem((BN, PIECE2, OWN), bf16),
-            vmem((BN, PIECE1, OWN), bf16),
-            vmem((BN, PIECE2, OWN), bf16),
+            vmem((BN, PIECE, OWN), bf16),
+            vmem((BN, PIECE, OWN), bf16),
+            vmem((3, SLICE, OWN), f32),
             vmem((2, ROWS, OWN), bf16),
             vmem((2 * ZN, 2, RES, OWN), bf16),
             vmem((2, ROWS, OWN), bf16),
@@ -504,9 +520,9 @@
             pltpu.SemaphoreType.REGULAR,
         ],
         compiler_params=pltpu.CompilerParams(
-            collective_id=0, has_side_effects=True, vmem_limit_bytes=60 * 1024 * 1024
+            collective_id=0, has_side_effects=True, vmem_limit_bytes=40 * 1024 * 1024
         ),
-    )(h, ids.reshape(1, ROWS), mask_index, k1, k2, w.T)
+    )(*(pltpu.with_memory_space_constraint(v, pltpu.HBM) for v in operands))
 
 
 def solution(mesh):

time: 60 us -> 54.1 us (0.902)
  Pallas kernels: 54.1 us -> 51 us
  local copies, waits for them, and re-layouts: 4.23 us -> 1.87 us
    pallas_call x1, Pallas kernels: 54.1 us -> 51 us  [local(): pl.pallas_call(kernel, out_shape=(jax.ShapeDtypeStruct((ROWS, CH), bf16),...]
    unnamed x3, local copies, waits for them, and re-layouts: 4.23 us -> 1.87 us
where the time goes in v4:
time: 54.1 us; the launch traced here: 53.5 us
  Pallas kernels  51 us (94%)
  local copies, waits for them, and re-layouts  1.87 us (3%)
  between operations  0.64 us (1%)
    pallas_call x1, Pallas kernels, local(): pl.pallas_call(kernel, out_shape=(jax.ShapeDtypeStruct((ROWS, CH), bf16),...  51 us
    unnamed x3, local copies, waits for them, and re-layouts  1.87 us

profile of v4, /device:TPU:1, one launch (start us, length us, event | category | flops | bytes accessed | tf_op | source)
XLA Modules:
  0.0 53.5 jit_solution(9592275137266787660)
XLA Ops:
  0.6 51.0 %shard_map.85 = (bf16[128,512]{1,0:T(8,128)(2,1)S(1)}, f32[9,4,128]{2,1,0:T(4,128)S(1)}, f32[9,4,128]{2,1,0:T(4,128)S(1)}) custom-call(bf16[128,512]{1,0:T(8,128)(2,1)} %h_ref.1, s32[1,128]{1,0:T(1,128)} %bitcast.3, s32[16]{0:T(128)} %mask_hbm.1, bf16[9,512,128]{2,1,0:T(8,128)(2,1)} %k1_hbm.1, bf16[9,512,128]{2,1,0:T(8,128)(2,1)} %k2_hbm.1, ...), custom_call_target="tpu_custom_call" | custom-call | tf_op jit(solution)/shard_map/pallas_call | solution.py:464
  51.6 0.7 %copy.12 = bf16[128,512]{1,0:T(8,128)(2,1)} copy(bf16[128,512]{1,0:T(8,128)(2,1)S(1)} %get-tuple-element.6) | data formatting | bytes 262144
  52.3 0.6 %copy.13 = f32[9,4,128]{2,1,0:T(4,128)} copy(f32[9,4,128]{2,1,0:T(4,128)S(1)} %get-tuple-element.7) | data formatting | bytes 36864
  52.9 0.6 %copy.14 = f32[9,4,128]{2,1,0:T(4,128)} copy(f32[9,4,128]{2,1,0:T(4,128)S(1)} %get-tuple-element.8) | data formatting | bytes 36864

commit v5 on v4

--- a/solution.py
+++ b/solution.py
@@ -16,10 +16,9 @@
 HOP1, HOP2 = 1, 2
 REACH1, REACH2 = 4, 3
 HALO1, HALO2 = REACH1 * HOP1, REACH2 * HOP2
-PIECE = 64
+PIECE1, PIECE2 = 48, 32
 AN, BN = 8, 16
 SLICE = CH // AN
-MODE = "cube"
 
 epsilon = 1e-05
 root_half = 0.7071067811865476
@@ -135,13 +134,13 @@
 
 def kernel(
     h_ref, ids_hbm, mask_hbm, k1_hbm, k2_hbm, w_hbm,
-    out_ref, dk1_hbm, dk2_hbm,
-    ids_ref, mask_ref, w_ref, dk1_ref, dk2_ref, k1, k2, hv, x0, x1, tsend, tgot, perm, w8, acc, wide,
+    out_ref, dk1_ref, dk2_ref,
+    ids_ref, mask_ref, w_ref, k1, k2, hv, x0, x1, tsend, tgot, perm, w8, acc, wide,
     act1, slope1, norm1, inv1, slope2, stat,
     hsend0, hsend1, ht0, ht1, d1, d2, dpad1, dpad2,
     psend1, psend2, pgot1, pgot2, rsend, rgot,
-    gsend, ggot, rest2, zsend, zgot, final,
-    send_sems, recv_sems, local_sems, ready_y, ready_x,
+    gsend, ggot, gsend2, ggot2, perm2, zsend, zgot, final,
+    send_sems, recv_sems, local_sems, ready_x,
 ):
     f32, bf16 = jnp.float32, jnp.bfloat16
     s, m = lax.axis_index("seq"), lax.axis_index("mp")
@@ -157,16 +156,10 @@
     core, xh = lax.rem(m, 2), m // 2
     cs = Group((core,), (2,), lambda c: (s, xh * 2 + c[0]))
     zx = Group((z, xh), (ZN, 2), lambda c: (seq_of(c[0], xl, y), c[1] * 2 + core))
-    if MODE == "cube":
-        z1, y1 = lax.rem(z, 2), lax.rem(y, 2)
-        z2, y2 = z // 2, y // 2
-        ga = Group((z1, xl, y1), (2, 2, 2), lambda c: (seq_of(z2 * 2 + c[0], c[1], y2 * 2 + c[2]), m))
-        gb = Group((z2, y2), (4, 4), lambda c: (seq_of(c[0] * 2 + z1, xl, c[1] * 2 + y1), m))
-        seq_at = lambda a, b: seq_of((b >> 2) * 2 + (a >> 2), (a >> 1) & 1, (b & 3) * 2 + (a & 1))
-    else:
-        ga = Group((z,), (ZN,), lambda c: (seq_of(c[0], xl, y), m))
-        gb = Group((xl, y), (XN, YN), lambda c: (seq_of(z, c[0], c[1]), m))
-        seq_at = lambda a, b: a * BN + b
+    ga = ys
+    gb = Group((z, xl), (ZN, XN), lambda c: (seq_of(c[0], c[1], y), m))
+    gb2 = Group((xl, y), (XN, YN), lambda c: (seq_of(z, c[0], c[1]), m))
+    seq_at = lambda a, b: seq_of(b >> 1, b & 1, a)
 
     count = itertools.count()
     started = []
@@ -182,8 +175,8 @@
                 device_id=device, device_id_type=MESH,
             )
 
-        def start(self, src_of, dst_of):
-            for off in self.group.offsets:
+        def start(self, src_of, dst_of, chosen=lambda off: True):
+            for off in filter(chosen, self.group.offsets):
                 to, device = self.group.to(off)
                 self.copy(src_of(to), dst_of(self.group.me()), device).start()
             if self not in started:
@@ -230,8 +223,7 @@
     move_h = Exchange(zs, x0.at[pl.ds(0, ROWS - RES)])
     move_h.start(lambda to: hv.at[rows16(to)], lambda me: x0.at[rows16(me)])
     x0[rows16(z), :] = hv[rows16(z), :]
-    for off in ys.offsets:
-        pl.semaphore_signal(ready_y, inc=1, device_id=ys.to(off)[1], device_id_type=MESH)
+    pl.semaphore_signal(ready_x, inc=1, device_id=xs.to((1,))[1], device_id_type=MESH)
 
     load_ids.wait()
     load_mask.wait()
@@ -252,8 +244,10 @@
     p = lax.broadcasted_iota(jnp.int32, (CH, 128), 0)
     a, b, low = p >> 6, (p >> 2) & (BN - 1), p & 3
     channel = seq_at(a, b) * 4 + low - lax.broadcasted_iota(jnp.int32, (CH, 128), 1)
+    same = p - lax.broadcasted_iota(jnp.int32, (CH, 128), 1)
     for i in range(CH // 128):
         perm[:, i * 128 : i * 128 + 128] = (channel == i * 128).astype(f32).astype(bf16)
+        perm2[:, i * 128 : i * 128 + 128] = (same == i * 128).astype(f32).astype(bf16)
 
     load_w.wait()
     w8[...] = jnp.concatenate([w_ref[...].astype(f32), jnp.zeros((8 - VOCAB, CH), f32)], axis=0)
@@ -272,13 +266,9 @@
     gather1 = Exchange(ms, act1.at[pl.ds(0, MN - 1)])
     gather1.start(lambda to: act1.at[m], lambda me: act1.at[me])
 
-    pl.semaphore_wait(ready_y, YN - 1)
-    pl.semaphore_signal(ready_x, inc=1, device_id=xs.to((1,))[1], device_id_type=MESH)
-
     mine = ga.me()
     hsend0[...] = nt(perm[...], x0[...]).astype(bf16)
     ht0[:, lanes(mine)] = hsend0[slices(mine), :]
-    pl.semaphore_wait(ready_x, XN - 1)
     move0 = Exchange(ga, ht0.at[:, pl.ds(0, (AN - 1) * ROWS)])
     move0.start(lambda to: hsend0.at[slices(to)], lambda me: ht0.at[:, lanes(me)])
     move_t.wait()
@@ -310,9 +300,9 @@
     share = Exchange(ms, stat.at[pl.ds(0, MN - 1)])
     share.start(lambda to: stat.at[m], lambda me: stat.at[me])
 
-    hsend1[...] = nt(perm[...], x1[...]).astype(bf16)
-    ht1[:, lanes(mine)] = hsend1[slices(mine), :]
-    move1 = Exchange(ga, ht1.at[:, pl.ds(0, (AN - 1) * ROWS)])
+    hsend1[...] = nt(perm2[...], x1[...]).astype(bf16)
+    ht1[:, lanes(z)] = hsend1[slices(z), :]
+    move1 = Exchange(zs, ht1.at[:, pl.ds(0, (AN - 1) * ROWS)])
     move1.start(lambda to: hsend1.at[slices(to)], lambda me: ht1.at[:, lanes(me)])
     own_logits = nt(w8[...].astype(bf16), x1[...])
     w_sum = jnp.sum(w8[...], axis=1, keepdims=True)
@@ -347,10 +337,10 @@
     dconv = by_row[:, 5:6] * (grad2 - by_row[:, 6:7] - values2 * by_row[:, 7:8]) * slope2[...]
     dconv = dconv.astype(bf16)
     d2[...] = dconv
-    dpad2[mine, HALO2 : HALO2 + ZN] = dconv.reshape(ZN, RES, OWN)
-
-    share2 = Exchange(ga, dpad2.at[pl.ds(0, AN - 1), pl.ds(HALO2, ZN)])
-    share2.start(lambda to: dpad2.at[mine, pl.ds(HALO2, ZN)], lambda me: dpad2.at[me, pl.ds(HALO2, ZN)])
+    dpad2[z, HALO2 : HALO2 + ZN] = dconv.reshape(ZN, RES, OWN)
+
+    share2 = Exchange(zs, dpad2.at[pl.ds(0, AN - 1), pl.ds(HALO2, ZN)])
+    share2.start(lambda to: dpad2.at[z, pl.ds(HALO2, ZN)], lambda me: dpad2.at[me, pl.ds(HALO2, ZN)])
 
     first = grad2
     second = grad2 * norm1[m]
@@ -398,11 +388,13 @@
 
     move1.wait()
     share2.wait()
-    owner = gb.me()
-    grads = tap_gradients(ht1, dpad2, HOP2, REACH2, HALO2)
-    pieces(grads[:4], gsend, 0)
-    for i in range(3):
-        rest2[i] = grads[4 + i]
+    owner, owner2 = gb.me(), gb2.me()
+    nothing = jnp.zeros((SLICE, OWN), f32)
+    pieces(tap_gradients(ht1, dpad2, HOP2, REACH2, HALO2) + [nothing], gsend2, 0)
+    ggot2[owner2] = gsend2[owner2]
+    pl.semaphore_wait(ready_x, XN - 1)
+    scatter2 = Exchange(gb2, ggot2.at[pl.ds(0, BN - 1)])
+    scatter2.start(lambda to: gsend2.at[to], lambda me: ggot2.at[me])
 
     reduce1.wait()
     for i in range(2):
@@ -413,8 +405,7 @@
 
     move0.wait()
     share1.wait()
-    grads = tap_gradients(ht0, dpad1, HOP1, REACH1, HALO1)
-    pieces([rest2[i] for i in range(3)] + grads, gsend, 16)
+    pieces(tap_gradients(ht0, dpad1, HOP1, REACH1, HALO1) + [nothing] * 3, gsend, 0)
     ggot[owner] = gsend[owner]
     scatter = Exchange(gb, ggot.at[pl.ds(0, BN - 1)])
     scatter.start(lambda to: gsend.at[to], lambda me: ggot.at[me])
@@ -433,24 +424,22 @@
 
     dk2_ref[0] = jnp.zeros((4, OWN), f32)
     dk2_ref[TAPS - 1] = jnp.zeros((4, OWN), f32)
+    scatter2.wait()
+    grads = ggot2[0].astype(f32)
+    for i in range(1, BN):
+        grads = grads + ggot2[i].astype(f32)
+    for j in range(2 * REACH2 + 1):
+        dk2_ref[MID - REACH2 + j] = grads[4 * j : 4 * j + 4]
     scatter.wait()
     grads = ggot[0].astype(f32)
     for i in range(1, BN):
         grads = grads + ggot[i].astype(f32)
-    for j in range(2 * REACH2 + 1):
-        dk2_ref[MID - REACH2 + j] = grads[4 * j : 4 * j + 4]
     for j in range(TAPS):
-        dk1_ref[j] = grads[28 + 4 * j : 32 + 4 * j]
-    store2 = pltpu.make_async_copy(dk2_ref, dk2_hbm, local_sems.at[7])
-    store1 = pltpu.make_async_copy(dk1_ref, dk1_hbm, local_sems.at[8])
-    store2.start()
-    store1.start()
+        dk1_ref[j] = grads[4 * j : 4 * j + 4]
 
     gather_out.wait()
     for copy in keep:
         copy.wait()
-    store2.wait()
-    store1.wait()
     for exchange in started:
         exchange.wait_send()
 
@@ -458,6 +447,7 @@
 def local(h, ids, mask_index, k1, k2, w):
     f32, bf16 = jnp.float32, jnp.bfloat16
     vmem = pltpu.VMEM
+    inside = pl.BlockSpec(memory_space=pltpu.VMEM)
     hbm = pl.BlockSpec(memory_space=pltpu.HBM)
     copies = 15
     operands = (h, ids.reshape(1, ROWS), mask_index, k1, k2, w.T)
@@ -469,13 +459,11 @@
             jax.ShapeDtypeStruct((TAPS, 4, OWN), f32),
         ),
         in_specs=[hbm] * 6,
-        out_specs=(hbm, hbm, hbm),
+        out_specs=(hbm, inside, inside),
         scratch_shapes=[
             vmem((1, ROWS), jnp.int32),
             pltpu.SMEM((16,), jnp.int32),
             vmem((VOCAB, CH), bf16),
-            vmem((TAPS, 4, OWN), f32),
-            vmem((TAPS, 4, OWN), f32),
             vmem((TAPS, CH, OWN), bf16),
             vmem((TAPS, CH, OWN), bf16),
             vmem((ROWS, CH), bf16),
@@ -507,16 +495,17 @@
             vmem((MN, ROWS, OWN), bf16),
             vmem((8, 128), f32),
             vmem((MN, 8, 128), f32),
-            vmem((BN, PIECE, OWN), bf16),
-            vmem((BN, PIECE, OWN), bf16),
-            vmem((3, SLICE, OWN), f32),
+            vmem((BN, PIECE1, OWN), bf16),
+            vmem((BN, PIECE1, OWN), bf16),
+            vmem((BN, PIECE2, OWN), bf16),
+            vmem((BN, PIECE2, OWN), bf16),
+            vmem((CH, CH), bf16),
             vmem((2, ROWS, OWN), bf16),
             vmem((2 * ZN, 2, RES, OWN), bf16),
             vmem((2, ROWS, OWN), bf16),
             pltpu.SemaphoreType.DMA((copies,)),
             pltpu.SemaphoreType.DMA((copies,)),
             pltpu.SemaphoreType.DMA((10,)),
-            pltpu.SemaphoreType.REGULAR,
             pltpu.SemaphoreType.REGULAR,
         ],
         compiler_params=pltpu.CompilerParams(

time: 54.1 us -> 51.7 us (0.956)
  Pallas kernels: 51 us -> 49.1 us
    pallas_call x1, Pallas kernels: 51 us -> 49.1 us  [local(): pl.pallas_call(kernel, out_shape=(jax.ShapeDtypeStruct((ROWS, CH), bf16),...]
where the time goes in v5:
time: 51.7 us; the launch traced here: 51.6 us
  Pallas kernels  49.1 us (95%)
  local copies, waits for them, and re-layouts  1.87 us (4%)
  between operations  0.64 us (1%)
    pallas_call x1, Pallas kernels, local(): pl.pallas_call(kernel, out_shape=(jax.ShapeDtypeStruct((ROWS, CH), bf16),...  49.1 us
    unnamed x3, local copies, waits for them, and re-layouts  1.87 us

profile of v5, /device:TPU:1, one launch (start us, length us, event | category | flops | bytes accessed | tf_op | source)
XLA Modules:
  0.0 51.6 jit_solution(17165847767830101304)
XLA Ops:
  0.6 49.1 %shard_map.85 = (bf16[128,512]{1,0:T(8,128)(2,1)S(1)}, f32[9,4,128]{2,1,0:T(4,128)S(1)}, f32[9,4,128]{2,1,0:T(4,128)S(1)}) custom-call(bf16[128,512]{1,0:T(8,128)(2,1)} %h_ref.1, s32[1,128]{1,0:T(1,128)} %bitcast.3, s32[16]{0:T(128)} %mask_hbm.1, bf16[9,512,128]{2,1,0:T(8,128)(2,1)} %k1_hbm.1, bf16[9,512,128]{2,1,0:T(8,128)(2,1)} %k2_hbm.1, ...), custom_call_target="tpu_custom_call" | custom-call | tf_op jit(solution)/shard_map/pallas_call | solution.py:454
  49.7 0.7 %copy.12 = bf16[128,512]{1,0:T(8,128)(2,1)} copy(bf16[128,512]{1,0:T(8,128)(2,1)S(1)} %get-tuple-element.6) | data formatting | bytes 262144
  50.4 0.6 %copy.13 = f32[9,4,128]{2,1,0:T(4,128)} copy(f32[9,4,128]{2,1,0:T(4,128)S(1)} %get-tuple-element.7) | data formatting | bytes 36864
  51.0 0.6 %copy.14 = f32[9,4,128]{2,1,0:T(4,128)} copy(f32[9,4,128]{2,1,0:T(4,128)S(1)} %get-tuple-element.8) | data formatting | bytes 36864

commit v6 on v5

--- a/solution.py
+++ b/solution.py
@@ -150,10 +150,10 @@
     seq_of = lambda z, x, y: (z * XN + x) * YN + y
 
     zs = Group((z,), (ZN,), lambda c: (seq_of(c[0], xl, y), m))
-    ms = Group((m,), (MN,), lambda c: (s, c[0]))
+    core, xh = lax.rem(m, 2), m // 2
+    ms = Group((xh, core), (2, 2), lambda c: (s, c[0] * 2 + c[1]))
     ys = Group((y,), (YN,), lambda c: (seq_of(z, xl, c[0]), m))
     xs = Group((xl,), (XN,), lambda c: (seq_of(z, c[0], y), m))
-    core, xh = lax.rem(m, 2), m // 2
     cs = Group((core,), (2,), lambda c: (s, xh * 2 + c[0]))
     zx = Group((z, xh), (ZN, 2), lambda c: (seq_of(c[0], xl, y), c[1] * 2 + core))
     ga = ys
@@ -345,13 +345,13 @@
     first = grad2
     second = grad2 * norm1[m]
     reduce2 = Exchange(ms, pgot2.at[pl.ds(0, MN - 1)])
-    for step in (2, 3, 1, 0):
-        i = lax.rem(m + step, MN)
+    for step in ms.offsets + [(0, 0)]:
+        i = ms.to(step)[0]
         back_conv_part(d2, k2, HOP2, REACH2, i, acc)
         part = acc[...].astype(bf16)
-        if step:
+        if any(step):
             psend2[i] = part
-            reduce2.start_one((step,), psend2.at[i], pgot2.at[m])
+            reduce2.start_one(step, psend2.at[i], pgot2.at[m])
         else:
             pgot2[m] = part
         part = part.astype(f32)

time: 51.7 us -> 52.4 us (1.014)
  Pallas kernels: 49.1 us -> 49.7 us
    pallas_call x1, Pallas kernels: 49.1 us -> 49.7 us  [local(): pl.pallas_call(kernel, out_shape=(jax.ShapeDtypeStruct((ROWS, CH), bf16),...]
where the time goes in v6:
time: 52.4 us; the launch traced here: 52.2 us
  Pallas kernels  49.7 us (95%)
  local copies, waits for them, and re-layouts  1.87 us (4%)
  between operations  0.64 us (1%)
    pallas_call x1, Pallas kernels, local(): pl.pallas_call(kernel, out_shape=(jax.ShapeDtypeStruct((ROWS, CH), bf16),...  49.7 us
    unnamed x3, local copies, waits for them, and re-layouts  1.87 us

profile of v6, /device:TPU:1, one launch (start us, length us, event | category | flops | bytes accessed | tf_op | source)
XLA Modules:
  0.0 52.2 jit_solution(17292357417412153309)
XLA Ops:
  0.6 49.7 %shard_map.85 = (bf16[128,512]{1,0:T(8,128)(2,1)S(1)}, f32[9,4,128]{2,1,0:T(4,128)S(1)}, f32[9,4,128]{2,1,0:T(4,128)S(1)}) custom-call(bf16[128,512]{1,0:T(8,128)(2,1)} %h_ref.1, s32[1,128]{1,0:T(1,128)} %bitcast.3, s32[16]{0:T(128)} %mask_hbm.1, bf16[9,512,128]{2,1,0:T(8,128)(2,1)} %k1_hbm.1, bf16[9,512,128]{2,1,0:T(8,128)(2,1)} %k2_hbm.1, ...), custom_call_target="tpu_custom_call" | custom-call | tf_op jit(solution)/shard_map/pallas_call | solution.py:454
  50.4 0.7 %copy.12 = bf16[128,512]{1,0:T(8,128)(2,1)} copy(bf16[128,512]{1,0:T(8,128)(2,1)S(1)} %get-tuple-element.6) | data formatting | bytes 262144
  51.0 0.6 %copy.13 = f32[9,4,128]{2,1,0:T(4,128)} copy(f32[9,4,128]{2,1,0:T(4,128)S(1)} %get-tuple-element.7) | data formatting | bytes 36864
  51.6 0.6 %copy.14 = f32[9,4,128]{2,1,0:T(4,128)} copy(f32[9,4,128]{2,1,0:T(4,128)S(1)} %get-tuple-element.8) | data formatting | bytes 36864
